TPU v7x, 128 devices: a whole 4x4x4 slice. The times are simulated.
128 devices in a mesh: sp: 8 (over x, y_lo), dp: 16 (over z, y_hi, core).
Axes of the slice: x: 4, y: 4 (y_hi: 2, y_lo: 2; y = y_hi * 2 + y_lo), z: 4, core: 2. Of those that a mesh axis runs over, the one named last changes fastest.
Arguments:
- queries: bfloat16 [16, 2048, 3072], P('dp', 'sp'), may hold values from -6 to 6
- keys: bfloat16 [16, 2048, 3072], P('dp', 'sp'), may hold values from -6 to 6
- values: bfloat16 [16, 2048, 3072], P('dp', 'sp'), may hold values from -6 to 6
- latents: float32 [16, 2048, 64], P('dp', 'sp'), may hold values from -6 to 6
- noise: float32 [16, 2048, 64], P('dp', 'sp'), may hold values from -6 to 6
- head_weight: bfloat16 [3072, 64], replicated, may hold values from -0.4375 to 0.4375
- adapter_down: bfloat16 [3072, 128], P(('sp', 'dp')), may hold values from -0.109375 to 0.109375
- adapter_up: bfloat16 [128, 64], replicated, may hold values from -0.5 to 0.5
- advantages: float32 [16], replicated, may hold values from -6 to 6
- lengths: int32 [16], replicated, may hold values from 1024 to 2048, as said below
- timesteps: int32 [16], replicated, may hold values from 0 to 15
- destinations: int32 [16, 8, 16, 1], P('dp', 'sp'), may hold values from 0 to 15; in each aligned block of 16 rows (0 to 15, 16 to 31, ..., all dimensions but the last counted through in order) at most 2 rows name the same one
Outputs:
- next_latents: float32 [16, 2048, 64], P('dp', 'sp')
- learner_delta: float32 [16, 8, 512, 64], P('dp', 'sp')
- ratios: float32 [16], replicated
- grad_adapter_down: float32 [3072, 128], P(('sp', 'dp'))
Inputs may be any that keep to these rules, and one draw needn't show every extreme that they name: `lengths`: every video has at least 1024 valid tokens; some video has exactly 2048. `destinations`: among the 16 blocks of one device no learner index appears more than 2 times, and some device reaches 2.
All inputs are finite; a program needn't handle non-finite values.
Results may differ from a plain program's by a relative error of at most 0.014.
Values may be sent and summed in bfloat16 or wider, within the bound.
A program may use at most 64 MiB of HBM per device.

v0:
```python
import jax
import jax.numpy as jnp
from jax import lax
from jax.sharding import PartitionSpec as P

HEAD_DIM = 128
CHANNELS = 64
ROWS_BLK = 16
STEPS = 16


ETA = 0.3
CLIP = 0.2
LOSS_SCALE = 4096.0
NORM_EPS = 1e-06


def plan(moments):
    level = 1.0 - moments.astype(jnp.float32) / STEPS
    step_size = jnp.float32(1.0 / STEPS)
    noise_scale = ETA * jnp.sqrt(step_size) * (0.5 + level)
    return (step_size, noise_scale)


def attend_head(query_head, key_head, value_head, live_keys):
    sequence = query_head.shape[0]
    block_rows = min(512, sequence)
    stacked = query_head.reshape(sequence // block_rows, block_rows, query_head.shape[1])

    def one_block(query_block):
        scores = jnp.dot(
            query_block, key_head.T, preferred_element_type=jnp.float32
        ) * query_head.shape[1] ** (-0.5)
        scores = jnp.where(live_keys[None, :], scores, -1e30)
        highest = jnp.max(scores, axis=1, keepdims=True)
        weights = jnp.exp(scores - highest)
        totals = jnp.sum(weights, axis=1, keepdims=True)
        mixed_block = (
            jnp.dot(weights.astype(jnp.bfloat16), value_head, preferred_element_type=jnp.float32)
            / totals
        )
        return mixed_block.astype(jnp.bfloat16)

    return lax.map(one_block, stacked).reshape(sequence, query_head.shape[1])


def normalize(feature_rows):
    wide = feature_rows.astype(jnp.float32)
    centre = jnp.mean(wide, axis=-1, keepdims=True)
    spread = jnp.mean((wide - centre) * (wide - centre), axis=-1, keepdims=True)
    return ((wide - centre) * lax.rsqrt(spread + NORM_EPS)).astype(jnp.bfloat16)


def objective(log_gains, advantages):
    ratios = jnp.exp(log_gains)
    clipped = jnp.clip(ratios, 1.0 - CLIP, 1.0 + CLIP)
    active = (ratios * advantages <= clipped * advantages).astype(jnp.float32)
    pull_video = -(LOSS_SCALE / advantages.shape[0]) * advantages * ratios * active
    return (ratios, pull_video)


def contract(normed_rows, block_piece):
    return jnp.dot(normed_rows, block_piece, preferred_element_type=jnp.float32)


def learner_step(adapter_codes, offset_rows, row_info, adapter_up, advantages):
    adapter_delta = jnp.dot(adapter_codes, adapter_up, preferred_element_type=jnp.float32)
    step_rows = row_info[:, 0]
    inverse_rows = row_info[:, 1]
    weight_rows = row_info[:, 2]
    owner_video = row_info[:, 3]
    new_offset = offset_rows - step_rows[:, None] * adapter_delta
    row_terms = (
        weight_rows
        * inverse_rows
        * jnp.sum(offset_rows * offset_rows - new_offset * new_offset, axis=1)
    )
    video_count = advantages.shape[0]
    member_of = (
        owner_video[:, None] == jnp.arange(video_count).astype(jnp.float32)[None, :]
    ).astype(jnp.float32)
    partial_gain = jnp.sum(member_of * row_terms[:, None], axis=0)
    log_gains = lax.psum(partial_gain, ("sp", "dp"))
    ratios, pull_video = objective(log_gains, advantages)
    pull_rows = jnp.sum(member_of * pull_video[None, :], axis=1)
    grad_delta = (
        (pull_rows * weight_rows * inverse_rows * 2.0 * step_rows)[:, None] * new_offset
    ).astype(jnp.bfloat16)
    grad_codes = jnp.dot(grad_delta, adapter_up.T, preferred_element_type=jnp.float32).astype(
        jnp.bfloat16
    )
    return (adapter_delta, grad_codes, ratios)


def on_device(
    queries,
    keys,
    values,
    latents,
    noise,
    head_weight,
    adapter_down,
    adapter_up,
    advantages,
    lengths,
    timesteps,
    destinations,
):
    local_rows = queries.shape[1]
    model_width = queries.shape[2]
    groups = lax.axis_size("sp")
    learners = lax.axis_size("dp")
    video_index = lax.axis_index("dp")
    member = lax.axis_index("sp")
    sequence = local_rows * groups
    local_heads = model_width // HEAD_DIM // groups
    length = lax.dynamic_index_in_dim(lengths, video_index, 0, False)
    moment = lax.dynamic_index_in_dim(timesteps, video_index, 0, False)
    step_size, noise_scale = plan(moment)
    live_keys = jnp.arange(sequence) < length
    query_split = queries[0].reshape(local_rows, groups, local_heads, HEAD_DIM)
    key_split = keys[0].reshape(local_rows, groups, local_heads, HEAD_DIM)
    value_split = values[0].reshape(local_rows, groups, local_heads, HEAD_DIM)
    query_part = lax.all_to_all(query_split, "sp", split_axis=1, concat_axis=0, tiled=True)
    key_part = lax.all_to_all(key_split, "sp", split_axis=1, concat_axis=0, tiled=True)
    value_part = lax.all_to_all(value_split, "sp", split_axis=1, concat_axis=0, tiled=True)

    def per_head(query_head, key_head, value_head):
        return attend_head(query_head, key_head, value_head, live_keys)

    mixed = jax.vmap(per_head, in_axes=(1, 1, 1), out_axes=1)(
        query_part[:, 0], key_part[:, 0], value_part[:, 0]
    )
    head_major = mixed[:, None]
    token_major = lax.all_to_all(head_major, "sp", split_axis=0, concat_axis=1, tiled=True)
    attention = token_major.reshape(local_rows, model_width)
    velocity = jnp.dot(attention, head_weight, preferred_element_type=jnp.float32)
    mean_old = latents[0] - step_size * velocity
    stepped = mean_old + noise_scale * noise[0]
    offset_rows = stepped - mean_old
    rows_live = (member * local_rows + jnp.arange(local_rows) < length).astype(jnp.float32)
    weight_rows = rows_live / (length.astype(jnp.float32) * CHANNELS)
    inverse = 1.0 / (2.0 * noise_scale * noise_scale)
    row_info = jnp.stack(
        [
            jnp.full((local_rows,), step_size),
            jnp.full((local_rows,), inverse),
            weight_rows,
            jnp.full((local_rows,), video_index.astype(jnp.float32)),
        ],
        axis=1,
    )
    blocks = local_rows // ROWS_BLK
    capacity = max(2, 2 * blocks // learners)
    slot_count = learners * capacity
    target = destinations[0, 0, :, 0]
    block_order = jnp.arange(blocks)
    before = (target[None, :] == target[:, None]) & (block_order[None, :] < block_order[:, None])
    slot_rank = jnp.sum(before.astype(jnp.int32), axis=1)
    slot_index = target * capacity + slot_rank
    placing = jnp.arange(slot_count)[:, None] == slot_index[None, :]
    placing_low = placing.astype(jnp.bfloat16)
    placing_wide = placing.astype(jnp.float32)

    def slots_wide(token_rows):
        moved = jnp.dot(
            placing_wide, token_rows.reshape(blocks, -1), precision=lax.Precision.HIGHEST
        )
        return moved.reshape(learners, capacity, ROWS_BLK, token_rows.shape[1])

    moved = jnp.dot(
        placing_low, attention.reshape(blocks, -1), preferred_element_type=jnp.float32
    ).astype(jnp.bfloat16)
    normed = normalize(
        lax.all_to_all(
            moved.reshape(learners, capacity, ROWS_BLK, attention.shape[1]),
            "dp",
            split_axis=0,
            concat_axis=0,
            tiled=True,
        ).reshape(-1, model_width)
    )
    adapter_codes = contract(
        normed, lax.all_gather(adapter_down, ("sp", "dp"), axis=0, tiled=True)
    ).astype(jnp.bfloat16)
    adapter_delta, grad_codes, ratios = learner_step(
        adapter_codes,
        lax.all_to_all(
            slots_wide(offset_rows).astype(jnp.bfloat16),
            "dp",
            split_axis=0,
            concat_axis=0,
            tiled=True,
        )
        .astype(jnp.float32)
        .reshape(-1, CHANNELS),
        lax.all_to_all(
            slots_wide(row_info).astype(jnp.bfloat16), "dp", split_axis=0, concat_axis=0, tiled=True
        )
        .astype(jnp.float32)
        .reshape(-1, 4),
        adapter_up,
        advantages,
    )
    grad_adapter_down = lax.psum_scatter(
        jnp.dot(normed.T, grad_codes, preferred_element_type=jnp.float32),
        ("sp", "dp"),
        scatter_dimension=0,
        tiled=True,
    )
    learner_delta = adapter_delta.reshape(1, 1, -1, CHANNELS)
    return (stepped[None], learner_delta, ratios, grad_adapter_down)


def solution(mesh):
    in_specs = (
        P("dp", "sp", None),
        P("dp", "sp", None),
        P("dp", "sp", None),
        P("dp", "sp", None),
        P("dp", "sp", None),
        P(),
        P(("sp", "dp"), None),
        P(),
        P(),
        P(),
        P(),
        P("dp", "sp", None, None),
    )
    out_specs = (P("dp", "sp", None), P("dp", "sp", None, None), P(), P(("sp", "dp"), None))
    return jax.shard_map(
        on_device, mesh=mesh, in_specs=in_specs, out_specs=out_specs, check_vma=False
    )
```

profile of v0, /device:TPU:1, one launch (start us, length us, event | category | flops | bytes accessed | tf_op | source)
XLA Modules:
  0.0 1149.7 jit_solution(2563569593722497269)
XLA Ops:
  9.9 5.9 all-to-all-start.1
  17.4 21.4 %all-to-all-done.1 = bf16[256,8,3,128]{0,3,2,1:T(8,128)(2,1)S(1)} async-done(((bf16[256,8,3,128]{0,3,2,1:T(8,128)(2,1)}), bf16[256,8,3,128]{0,3,2,1:T(8,128)(2,1)S(1)}, u32[]{:S(2)}, u32[]{:S(2)}) %all-to-all-start.1) | async-done | bytes 1572896 | tf_op jit(solution)/shard_map/all_to_all | solution.py:125
  38.8 3.6 all-to-all-start.2
  45.0 19.5 %all-to-all-done.2 = bf16[256,8,3,128]{0,3,2,1:T(8,128)(2,1)S(1)} async-done(((bf16[256,8,3,128]{0,3,2,1:T(8,128)(2,1)}), bf16[256,8,3,128]{0,3,2,1:T(8,128)(2,1)S(1)}, u32[]{:S(2)}, u32[]{:S(2)}) %all-to-all-start.2) | async-done | bytes 1572896 | tf_op jit(solution)/shard_map/all_to_all | solution.py:126
  64.5 4.3 all-to-all-start
  74.3 16.2 %all-to-all-done = bf16[256,8,3,128]{0,3,2,1:T(8,128)(2,1)} async-done(((bf16[256,8,3,128]{0,3,2,1:T(8,128)(2,1)}), bf16[256,8,3,128]{0,3,2,1:T(8,128)(2,1)}, u32[]{:S(2)}, u32[]{:S(2)}) %all-to-all-start) | async-done | bytes 1572896 | tf_op jit(solution)/shard_map/all_to_all | solution.py:124
  92.3 37.2 %while.11 = (s32[]{:T(128)}, bf16[4,3,512,128]{3,2,0,1:T(8,128)(2,1)}, bf16[4,3,512,128]{3,2,0,1:T(8,128)(2,1)S(1)}, bf16[2048,3,128]{0,2,1:T(8,128)(2,1)S(1)}, ...) while((s32[]{:T(128)}, bf16[4,3,512,128]{3,2,0,1:T(8,128)(2,1)}, ...), condition=%wide.region_3.4_spmd.clone, body=%wide.region_0.3_spmd.clone.sunk | while | flops 1645607936 | bytes 48011888 | solution.py:44
  98.0 3.6 fusion.71
  107.3 3.6 fusion.71
  116.6 3.6 fusion.71
  125.9 3.6 fusion.71
  129.6 4.2 copy.135
  133.7 3.7 all-to-all-start.3
  141.8 24.6 %all-to-all-done.3 = bf16[2048,1,3,128]{3,2,1,0:T(4,128)(2,1)S(1)} async-done(((bf16[2048,1,3,128]{3,2,1,0:T(4,128)(2,1)}), bf16[2048,1,3,128]{3,2,1,0:T(4,128)(2,1)S(1)}, u32[]{:S(2)}, u32[]{:S(2)}) %all-to-all-start.3) | async-done | bytes 1572896 | tf_op jit(solution)/shard_map/all_to_all | solution.py:135
  167.8 9.9 all-to-all-start.5
  189.8 7.2 all-to-all-start.6
  197.9 3.3 copy.155
  204.9 4.2 all-to-all-start.4
  209.7 212.5 %all_gather.3 = bf16[3072,128]{1,0:T(8,128)(2,1)} all-gather(bf16[24,128]{1,0:T(8,128)(2,1)S(1)} %copy-done.10), channel_id=1, replica_groups=mesh['sp'=8,'dp'=16] {'sp','dp'}, dimensions={0}, use_global_device_ids=true | all-gather | bytes 792576 | tf_op jit(solution)/shard_map/all_gather | solution.py:184
  433.1 3.7 fusion.28
  436.8 4.7 subtract_reduce_fusion
  443.5 62.2 %psum.7 = f32[16]{0:T(128)} all-reduce(f32[16]{0:T(128)} %fusion.38), channel_id=1, replica_groups=mesh['sp'=8,'dp'=16] {'sp','dp'}, use_global_device_ids=true, to_apply=%region_9.10 | all-reduce | flops 16 | bytes 128 | tf_op jit(solution)/shard_map/psum | solution.py:83
  507.6 3.4 fusion.30
  511.0 631.9 %reduce-scatter.5.cloned.1.call-done = f32[24,128]{1,0:T(8,128)} async-done(((f32[3072,128]{1,0:T(8,128)}), f32[24,128]{1,0:T(8,128)}) %reduce-scatter.5.cloned.1.call-update) | async-done | bytes 12304
  (104 shorter events, 73.0 us)
Async XLA Ops:
  7.2 173.0 %copy-start = (bf16[3072,64]{0,1:T(8,128)(2,1)S(1)}, bf16[3072,64]{0,1:T(8,128)(2,1)}, u32[]{:S(2)}) copy-start(bf16[3072,64]{0,1:T(8,128)(2,1)} %param.19) | copy-start | bytes 1179652
  7.2 8.6 copy-start.3
  9.9 28.9 %all-to-all-start.1 = ((bf16[256,8,3,128]{0,3,2,1:T(8,128)(2,1)}), bf16[256,8,3,128]{0,3,2,1:T(8,128)(2,1)S(1)}, u32[]{:S(2)}, u32[]{:S(2)}) async-start(bf16[256,8,3,128]{0,3,2,1:T(8,128)(2,1)} %bitcast.8), calls=%async_computation.1 | async-start | bytes 3145728 | tf_op jit(solution)/shard_map/all_to_all | solution.py:125
  38.8 25.6 %all-to-all-start.2 = ((bf16[256,8,3,128]{0,3,2,1:T(8,128)(2,1)}), bf16[256,8,3,128]{0,3,2,1:T(8,128)(2,1)S(1)}, u32[]{:S(2)}, u32[]{:S(2)}) async-start(bf16[256,8,3,128]{0,3,2,1:T(8,128)(2,1)} %bitcast.137), calls=%async_computation.2 | async-start | bytes 3145728 | tf_op jit(solution)/shard_map/all_to_all | solution.py:126
  42.4 26.4 %copy-start.11 = (s32[16]{0:T(128)S(1)}, s32[16]{0:T(128)}, u32[]{:S(2)}) copy-start(s32[16]{0:T(128)} %param.23) | copy-start | bytes 196
  64.5 26.0 %all-to-all-start = ((bf16[256,8,3,128]{0,3,2,1:T(8,128)(2,1)}), bf16[256,8,3,128]{0,3,2,1:T(8,128)(2,1)}, u32[]{:S(2)}, u32[]{:S(2)}) async-start(bf16[256,8,3,128]{0,3,2,1:T(8,128)(2,1)} %bitcast.136), calls=%async_computation | async-start | bytes 3145728 | tf_op jit(solution)/shard_map/all_to_all | solution.py:124
  95.2 2.8 copy-start.4
  104.5 2.8 copy-start.4
  113.8 2.8 copy-start.4
  123.1 2.8 copy-start.4
  129.6 8.6 copy-start.12
  133.7 7.0 copy-start.13
  133.7 32.7 %all-to-all-start.3 = ((bf16[2048,1,3,128]{3,2,1,0:T(4,128)(2,1)}), bf16[2048,1,3,128]{3,2,1,0:T(4,128)(2,1)S(1)}, u32[]{:S(2)}, u32[]{:S(2)}) async-start(bf16[2048,1,3,128]{3,2,1,0:T(4,128)(2,1)} %copy.135), calls=%async_computation.3 | async-start | bytes 4194304 | tf_op jit(solution)/shard_map/all_to_all | solution.py:135
  166.4 1.3 copy-start.2
  167.8 22.0 %all-to-all-start.5 = ((bf16[16,2,16,4]{2,3,1,0:T(4,128)(2,1)}), bf16[16,2,16,4]{2,3,1,0:T(4,128)(2,1)}, u32[]{:S(2)}, u32[]{:S(2)}) async-start(bf16[16,2,16,4]{2,3,1,0:T(4,128)(2,1)} %copy.142), calls=%async_computation.5 | async-start | bytes 65536 | tf_op jit(solution)/shard_map/all_to_all | solution.py:197
  189.8 14.6 %all-to-all-start.6 = ((bf16[16,2,1024]{2,1,0:T(2,128)(2,1)}), bf16[16,2,1024]{2,1,0:T(2,128)(2,1)S(1)}, u32[]{:S(2)}, u32[]{:S(2)}) async-start(bf16[16,2,1024]{2,1,0:T(2,128)(2,1)} %reshape.183), calls=%async_computation.6 | async-start | bytes 131072 | tf_op jit(solution)/shard_map/all_to_all | solution.py:188
  204.3 5.4 copy-start.10
  204.9 225.3 %all-to-all-start.4 = ((bf16[16,2,16,3072]{3,2,1,0:T(8,128)(2,1)}), bf16[16,2,16,3072]{3,2,1,0:T(8,128)(2,1)S(1)}, u32[]{:S(2)}, u32[]{:S(2)}) async-start(bf16[16,2,16,3072]{3,2,1,0:T(8,128)(2,1)} %bitcast.131), calls=%async_computation.4 | async-start | bytes 6291456 | tf_op jit(solution)/shard_map/all_to_all | solution.py:175
  209.1 933.7 %reduce-scatter.5.cloned.1.call-start = ((), (), s32[]{:S(2)}) async-start(), calls=%async_computation.8 | async-start | bytes 1585152
  424.7 5.6 copy-start.6
  433.1 3.7 copy-start.9
  436.8 4.7 copy-start.7
  436.8 5.4 copy-start.8
  436.8 70.8 %copy-start.1 = (bf16[512,3072]{1,0:T(8,128)(2,1)S(1)}, bf16[512,3072]{1,0:T(8,128)(2,1)}, u32[]{:S(2)}) copy-start(bf16[512,3072]{1,0:T(8,128)(2,1)} %fusion.28) | copy-start | bytes 9437188
  (1 other events, 0.6 us)
Sparse Core Ops, SparseCore 0:
  511.1 631.6 reduce-scatter.4
where the time goes:
time: 1160 us; the launch traced here: 1150 us
  waiting for transfers between devices  717 us (62%)
  blocking collectives  275 us (24%)
  local copies, waits for them, and re-layouts  42.2 us (4%)
  starting transfers between devices  38.8 us (3%)
  matrix products  34.7 us (3%)
  other arithmetic  26.9 us (2%)
  between operations  15.7 us (1%)
    unnamed x2, waiting for transfers between devices  632 us
    all_gather x1, blocking collectives, on_device(): lax.all_gather(adapter_down, ('sp', 'dp'), axis=0, tiled=True)  213 us
    psum x1, blocking collectives, learner_step(): log_gains = lax.psum(partial_gain, ('sp', 'dp'))  62.2 us
    all_to_all x1, waiting for transfers between devices, on_device(): lax.all_to_all(head_major, 'sp', split_axis=0, concat_axis=1, tiled=True)  24.6 us
  transfers between devices with their start and end apart: 8, of which 6 were waited for; matrix products, arithmetic and copies ran while one was open for 3% of the time, Pallas kernels for 0%

commit v1 on v0

v1 whole, which is shorter than its diff:
```python
import functools

import jax
import jax.numpy as jnp
from jax import lax
from jax.experimental import pallas as pl
from jax.experimental.pallas import tpu as pltpu
from jax.sharding import PartitionSpec as P

MESH = pl.DeviceIdType.MESH
F32 = jnp.float32
BF16 = jnp.bfloat16

HD = 128
CH = 64
STEPS = 16
ETA = 0.3
CLIP = 0.2
LOSS_SCALE = 4096.0
NORM_EPS = 1e-06
NSP = 8
NDP = 16
ROWS = 256
SEQ = 2048
HEADS = 3
FEAT = HEADS * HD
OWN = 24
LOG2E = 1.4426950408889634
STEP = 1.0 / STEPS

OFFSETS = ((2, 1), (2, 0), (1, 1), (3, 1), (1, 0), (3, 0), (0, 1))
NP = len(OFFSETS)


def nt(a, b):
    return lax.dot_general(a, b, (((1,), (1,)), ((), ())), preferred_element_type=F32)


def tn(a, b):
    return lax.dot_general(a, b, (((0,), (0,)), ((), ())), preferred_element_type=F32)


def nn(a, b):
    return jnp.dot(a, b, preferred_element_type=F32)


def kernel(
    q_hbm, k_hbm, v_hbm, lat_hbm, noise_hbm, hw_hbm, ad_ref, up_ref, adv_ref, len_ref, time_ref, dest_ref,
    next_ref, learn_ref, ratio_ref, grad_ref,
    qland, kland, vland, att, lat, noise, wt, hw, piece, wg, cs_out, cs_in, csb, hwb,
    r1s, r1r, r2, slots, learn_in, g_out, g_in,
    loc_sem, s0, r0, sa, ra, sc, rc, s1, r1, s2, rr2, sl, rl, s3, r3,
):
    me = lax.axis_index("sp")
    vid = lax.axis_index("dp")
    mx, my = me // 2, me % 2

    def peer(i):
        dx, dy = OFFSETS[i]
        return ((mx + dx) % 4) * 2 + (my + dy) % 2

    def source(i):
        dx, dy = OFFSETS[i]
        return ((mx + 4 - dx) % 4) * 2 + (my + 2 - dy) % 2

    def dp_peer(e):
        return (vid + e) % NDP

    def dp_source(e):
        return (vid + NDP - e) % NDP

    def rows_of(s):
        return pl.ds(pl.multiple_of(s * ROWS, ROWS), ROWS)

    def columns_of(s, h):
        return pl.ds(pl.multiple_of(s * FEAT + h * HD, HD), HD)

    barrier = pltpu.get_barrier_semaphore()
    for i in range(NP):
        pl.semaphore_signal(barrier, inc=1, device_id=(peer(i), vid), device_id_type=MESH)
    for e in range(1, NDP):
        pl.semaphore_signal(barrier, inc=1, device_id=(me, dp_peer(e)), device_id_type=MESH)

    sources = (k_hbm, q_hbm, v_hbm)

    def landing(t, h, s):
        if t == 2:
            return vland.at[h, rows_of(s), pl.ds(0, HD)]
        return (kland, qland)[t].at[h, rows_of(s), :]

    local = []
    for g in range(9):
        h, t = g // 3, g % 3
        local.append(
            pltpu.make_async_copy(sources[t].at[0, :, columns_of(me, h)], landing(t, h, me), loc_sem.at[g])
        )
    hw_copy = pltpu.make_async_copy(
        hw_hbm.at[:, pl.ds(pl.multiple_of(me * FEAT, HD), FEAT)], hw, loc_sem.at[9]
    )
    lat_copy = pltpu.make_async_copy(lat_hbm, lat, loc_sem.at[10])
    noise_copy = pltpu.make_async_copy(noise_hbm, noise, loc_sem.at[11])
    extra = [hw_copy, lat_copy, noise_copy]

    pl.semaphore_wait(barrier, NP + NDP - 1)

    order = (0, 1, 2, 3, 4, 5, 6, 8, 7)
    groups = []
    for g in order:
        h, t = g // 3, g % 3
        groups.append(
            [
                pltpu.make_async_remote_copy(
                    src_ref=sources[t].at[0, :, columns_of(peer(i), h)],
                    dst_ref=landing(t, h, me),
                    send_sem=s0.at[g, i],
                    recv_sem=r0.at[g, i],
                    device_id=(peer(i), vid),
                    device_id_type=MESH,
                )
                for i in range(NP)
            ]
        )

    def issue(n):
        for c in groups[n]:
            c.start()

    def sent(n):
        for c in groups[n]:
            c.wait_send()

    def arrived(n):
        for c in groups[n]:
            c.wait_recv()

    for n in range(3):
        issue(n)
    for c in local + extra:
        c.start()

    up = up_ref[...]
    up_low = jnp.concatenate([jnp.zeros_like(up), up], axis=0)
    piece[...] = nt(ad_ref[...], up_low)
    own_rows = pl.ds(pl.multiple_of(vid * OWN, 8), OWN)
    gather = [
        pltpu.make_async_remote_copy(
            src_ref=piece,
            dst_ref=wg.at[own_rows, :],
            send_sem=sa.at[e],
            recv_sem=ra.at[e],
            device_id=(me, dp_peer(e)),
            device_id_type=MESH,
        )
        for e in range(1, NDP)
    ]
    for c in gather:
        c.start()
    wg[own_rows, :] = piece[...]
    for h in range(HEADS):
        vland[h, :, HD:] = jnp.ones((SEQ, HD), BF16)
    hw_copy.wait()
    for c in gather:
        c.wait()
    wt[0:CH, :] = hw[...]
    wt[CH:, :] = jnp.transpose(wg[...])[CH:, :].astype(BF16)
    ones = jnp.ones((16, FEAT), BF16)
    cs_out[...] = nt(ones, wt[...])[0:8]
    cs_copies = [
        pltpu.make_async_remote_copy(
            src_ref=cs_out,
            dst_ref=cs_in.at[i],
            send_sem=sc.at[i],
            recv_sem=rc.at[i],
            device_id=(peer(i), vid),
            device_id_type=MESH,
        )
        for i in range(NP)
    ]
    for c in cs_copies:
        c.start()
    cs_in[NP] = cs_out[...]
    for c in cs_copies:
        c.wait()
    for i in range(NP + 1):
        spread = jnp.transpose(jnp.broadcast_to(cs_in[i][0:1], (HD, HD)))
        csb[i] = spread[CH:]
        if i == NP:
            hwb[...] = spread[:CH]

    length = len_ref[vid]
    moment = time_ref[vid].astype(F32)
    noise_scale = jnp.full((1, ROWS), (ETA * 0.25) * (0.5 + (1.0 - moment * STEP)), F32)
    inverse = 1.0 / (2.0 * noise_scale * noise_scale)
    token = me * ROWS + lax.broadcasted_iota(jnp.int32, (1, ROWS), 1)
    live = jnp.where(token < length, 1.0, 0.0).astype(F32)
    row_weight = live / (jnp.full((1, ROWS), length.astype(F32), F32) * CH)
    gain = row_weight * inverse
    key_at = SEQ // 2 + lax.broadcasted_iota(jnp.int32, (1, SEQ // 2), 1)
    cap = jnp.where(key_at < length, 3e38, -1e30).astype(F32)

    def attend(h, rows):
        scores = nt(qland[h, rows, :], kland[h]) * (LOG2E * HD**-0.5)
        first = scores[:, : SEQ // 2]
        second = jnp.minimum(scores[:, SEQ // 2 :], cap)
        highest = jnp.maximum(
            jnp.max(first, axis=1, keepdims=True), jnp.max(second, axis=1, keepdims=True)
        )
        low = jnp.exp2(first - highest).astype(BF16)
        high = jnp.exp2(second - highest).astype(BF16)
        mixed = nn(jnp.concatenate([low, high], axis=1), vland[h])
        att[rows, h * HD : (h + 1) * HD] = (mixed[:, :HD] / mixed[:, HD:]).astype(BF16)

    def attend_all(h):
        @pl.loop(0, NSP)
        def _(b):
            attend(h, rows_of(b))

    for c in local + [lat_copy, noise_copy]:
        c.wait()
    for h in range(2):
        for t in range(3):
            n = h * 3 + t
            sent(n)
            issue(n + 3)
            arrived(n)
        attend_all(h)

    for n in (6, 7):
        arrived(n)

    def partial_sums(rows):
        feature = att[rows, :]
        wide = feature.astype(F32)
        centred = wide - jnp.sum(wide, axis=1, keepdims=True) * (1.0 / FEAT)
        sums = nt(wt[...], centred.astype(BF16))
        mean = nt(ones, feature) * (1.0 / FEAT)
        square = nt(ones, (centred * centred).astype(BF16))
        spread = jnp.concatenate([hwb[...], hwb[...]], axis=1)
        velocity = sums[:CH] + spread * mean[0:1]
        line = lax.broadcasted_iota(jnp.int32, (16, ROWS), 0)
        mean_high = mean.astype(BF16).astype(F32)
        square_high = square.astype(BF16).astype(F32)
        stats = jnp.where(
            line == 0,
            mean_high,
            jnp.where(line == 1, mean - mean_high, jnp.where(line == 2, square_high, square - square_high)),
        )
        return jnp.concatenate([velocity, sums[CH:], stats], axis=0).astype(BF16)

    part_copies = [
        pltpu.make_async_remote_copy(
            src_ref=r1s.at[i],
            dst_ref=r1r.at[i],
            send_sem=s1.at[i],
            recv_sem=r1.at[i],
            device_id=(peer(i), vid),
            device_id_type=MESH,
        )
        for i in range(NP)
    ]
    opposite = [OFFSETS.index(((4 - dx) % 4, (2 - dy) % 2)) for dx, dy in OFFSETS]
    for i in range(NP):
        groups[8][opposite[i]].wait_recv()
        rows = rows_of(peer(i))
        attend(2, rows)
        r1s[i] = partial_sums(rows)
        part_copies[i].start()
    attend(2, rows_of(me))
    r1r[NP] = partial_sums(rows_of(me))
    for n in (6, 7, 8):
        sent(n)
    for c in part_copies:
        c.wait()

    parts = [r1r[i].astype(F32) for i in range(NP + 1)]
    total = parts[0][: 2 * CH]
    for p in parts[1:]:
        total = total + p[: 2 * CH]
    means = [p[128:129] + p[129:130] for p in parts]
    squares = [p[130:131] + p[131:132] for p in parts]
    mean = functools.reduce(jnp.add, means) * (1.0 / NSP)
    gaps = [m - mean for m in means]
    variance = functools.reduce(jnp.add, squares) + FEAT * functools.reduce(jnp.add, [g * g for g in gaps])
    rstd = lax.rsqrt(variance * (1.0 / (FEAT * NSP)) + NORM_EPS)
    inner = total[CH:]
    for i in range(NP + 1):
        inner = inner + jnp.concatenate([csb[i], csb[i]], axis=1) * gaps[i]
    delta = inner * rstd
    offset = noise_scale * noise[...]
    gap = offset - STEP * delta
    unit = (gap * (gain * (2.0 * STEP) * rstd)).astype(BF16)
    terms = gain * jnp.sum(offset * offset - gap * gap, axis=0, keepdims=True)
    line = lax.broadcasted_iota(jnp.int32, (16, ROWS), 0)
    mean_high = mean.astype(BF16).astype(F32)
    terms_high = terms.astype(BF16).astype(F32)
    terms_rest = terms - terms_high
    terms_mid = terms_rest.astype(BF16).astype(F32)
    side = jnp.where(line == 0, mean_high, jnp.where(line == 1, mean - mean_high, 0.0))
    side = jnp.where(line == 2, terms_high, side)
    side = jnp.where(line == 3, terms_mid, jnp.where(line == 4, terms_rest - terms_mid, side))
    r2[me, 0:CH] = unit
    r2[me, CH : CH + 16] = side.astype(BF16)
    unit_copies = [
        pltpu.make_async_remote_copy(
            src_ref=r2.at[me],
            dst_ref=r2.at[me],
            send_sem=s2.at[i],
            recv_sem=rr2.at[i],
            device_id=(peer(i), vid),
            device_id_type=MESH,
        )
        for i in range(NP)
    ]
    for c in unit_copies:
        c.start()

    lane = lax.broadcasted_iota(jnp.int32, (1, ROWS), 1)
    targets = [dest_ref[0, b] for b in range(16)]
    place = jnp.zeros((1, ROWS), jnp.int32)
    for b in range(16):
        rank = jnp.int32(0)
        for a in range(b):
            rank = rank + jnp.where(targets[a] == targets[b], 1, 0)
        place = jnp.where(lane // 16 == b, targets[b] * 2 + rank, place)
    place = place * 16 + lane % 16
    placing = (lax.broadcasted_iota(jnp.int32, (512, ROWS), 0) == place).astype(F32).astype(BF16)
    delta_low = delta.astype(BF16)
    slots[...] = nt(placing, jnp.concatenate([delta_low, jnp.zeros_like(delta_low)], axis=0)).astype(BF16)
    mine = pl.ds(pl.multiple_of(vid * 32, 32), 32)
    learn_copies = [
        pltpu.make_async_remote_copy(
            src_ref=slots.at[pl.ds(pl.multiple_of(dp_peer(e) * 32, 32), 32), :],
            dst_ref=learn_in.at[mine, :],
            send_sem=sl.at[e],
            recv_sem=rl.at[e],
            device_id=(me, dp_peer(e)),
            device_id_type=MESH,
        )
        for e in range(1, NDP)
    ]
    for c in learn_copies:
        c.start()
    learn_in[mine, :] = slots[mine, :]
    next_ref[...] = (lat[...] - STEP * total[:CH]) + offset

    def grad_part(s):
        u = r2[s, 0:CH]
        side = r2[s, CH : CH + 16]
        shift = nt(u, side)
        return nn(u, att[rows_of(s), :]) - (shift[:, 0:1] + shift[:, 1:2])

    grad = grad_part(me)
    for i in range(NP):
        unit_copies[i].wait_recv()
        grad = grad + grad_part(source(i))
    sides = r2[0, CH : CH + 16].astype(F32)
    for s in range(1, NSP):
        sides = sides + r2[s, CH : CH + 16].astype(F32)
    log_gain = jnp.sum(sides[2:3] + sides[3:4] + sides[4:5], axis=1, keepdims=True)
    log_gain = jnp.broadcast_to(log_gain, (8, HD))
    ratio = jnp.exp(log_gain)
    advantage = adv_ref[vid]
    clipped = jnp.clip(ratio, 1.0 - CLIP, 1.0 + CLIP)
    active = jnp.where(ratio * advantage <= clipped * advantage, 1.0, 0.0)
    pull = -(LOSS_SCALE / NDP) * advantage * ratio * active
    grad_high = grad.astype(BF16)
    grad_rest = (grad - grad_high.astype(F32)).astype(BF16)
    product = tn(jnp.concatenate([grad_high, grad_rest], axis=0), jnp.concatenate([up, up], axis=0))
    product = product * pull[0:1]
    for k in range(NDP):
        g_out[k, 0:OWN] = product[k * OWN : (k + 1) * OWN]
        g_out[k, OWN : OWN + 8] = log_gain
    grad_copies = [
        pltpu.make_async_remote_copy(
            src_ref=g_out.at[dp_peer(e)],
            dst_ref=g_in.at[vid],
            send_sem=s3.at[e],
            recv_sem=r3.at[e],
            device_id=(me, dp_peer(e)),
            device_id_type=MESH,
        )
        for e in range(1, NDP)
    ]
    for c in grad_copies:
        c.start()
    g_in[vid] = g_out[vid]

    for c in learn_copies:
        c.wait()
    select = lax.broadcasted_iota(jnp.int32, (CH, HD), 0) == lax.broadcasted_iota(jnp.int32, (CH, HD), 1)
    learn_ref[...] = nt(select.astype(F32).astype(BF16), learn_in[...])
    for c in unit_copies:
        c.wait_send()

    for c in grad_copies:
        c.wait()
    summed = g_in[0, 0:OWN]
    for k in range(1, NDP):
        summed = summed + g_in[k, 0:OWN]
    grad_ref[...] = summed
    column = lax.broadcasted_iota(jnp.int32, (8, HD), 1)
    gains = jnp.zeros((8, HD), F32)
    for k in range(NDP):
        gains = jnp.where(column == k, g_in[k, OWN : OWN + 8], gains)
    ratio_ref[...] = jnp.exp(gains)


def on_device(
    queries, keys, values, latents, noise, head_weight, adapter_down, adapter_up, advantages, lengths, timesteps,
    destinations,
):
    hbm = pl.BlockSpec(memory_space=pl.ANY)
    vmem = pl.BlockSpec(memory_space=pltpu.VMEM)
    smem = pl.BlockSpec(memory_space=pltpu.SMEM)
    dma = pltpu.SemaphoreType.DMA
    nxt, learn, ratio, grad = pl.pallas_call(
        kernel,
        out_shape=(
            jax.ShapeDtypeStruct((CH, ROWS), F32),
            jax.ShapeDtypeStruct((CH, 512), F32),
            jax.ShapeDtypeStruct((8, HD), F32),
            jax.ShapeDtypeStruct((OWN, HD), F32),
        ),
        in_specs=[hbm] * 6 + [vmem] * 2 + [smem] * 4,
        out_specs=(vmem,) * 4,
        scratch_shapes=[
            pltpu.VMEM((HEADS, SEQ, HD), BF16),
            pltpu.VMEM((HEADS, SEQ, HD), BF16),
            pltpu.VMEM((HEADS, SEQ, 2 * HD), BF16),
            pltpu.VMEM((SEQ, FEAT), BF16),
            pltpu.VMEM((CH, ROWS), F32),
            pltpu.VMEM((CH, ROWS), F32),
            pltpu.VMEM((2 * CH, FEAT), BF16),
            pltpu.VMEM((CH, FEAT), BF16),
            pltpu.VMEM((OWN, HD), F32),
            pltpu.VMEM((FEAT, HD), F32),
            pltpu.VMEM((8, HD), F32),
            pltpu.VMEM((NSP, 8, HD), F32),
            pltpu.VMEM((NSP, CH, HD), F32),
            pltpu.VMEM((CH, HD), F32),
            pltpu.VMEM((NP, 144, ROWS), BF16),
            pltpu.VMEM((NSP, 144, ROWS), BF16),
            pltpu.VMEM((NSP, CH + 16, ROWS), BF16),
            pltpu.VMEM((512, HD), BF16),
            pltpu.VMEM((512, HD), BF16),
            pltpu.VMEM((NDP, OWN + 8, HD), F32),
            pltpu.VMEM((NDP, OWN + 8, HD), F32),
            dma((12,)),
            dma((9, NP)), dma((9, NP)),
            dma((NDP,)), dma((NDP,)),
            dma((NP,)), dma((NP,)),
            dma((NP,)), dma((NP,)),
            dma((NP,)), dma((NP,)),
            dma((NDP,)), dma((NDP,)),
            dma((NDP,)), dma((NDP,)),
        ],
        compiler_params=pltpu.CompilerParams(
            collective_id=0, has_side_effects=True, vmem_limit_bytes=56 * 2**20
        ),
        cost_estimate=pl.CostEstimate(
            flops=7 * 10**9, bytes_accessed=6 * 10**6, transcendentals=13 * 10**6
        ),
        name="policy_step",
    )(
        queries, keys, values, latents[0].T, noise[0].T, head_weight.T, adapter_down, adapter_up.T, advantages,
        lengths, timesteps, destinations.reshape(1, 16),
    )
    return nxt.T[None], learn.T[None, None], ratio[0, :NDP], grad


def solution(mesh):
    wide = P("dp", "sp", None)
    in_specs = (
        wide, wide, wide, wide, wide, P(), P(("sp", "dp"), None), P(), P(), P(), P(), P("dp", "sp", None, None),
    )
    out_specs = (wide, P("dp", "sp", None, None), P(), P(("sp", "dp"), None))
    return jax.shard_map(on_device, mesh=mesh, in_specs=in_specs, out_specs=out_specs, check_vma=False)
```

time: 1160 us -> 110 us (0.09)
  waiting for transfers between devices: 717 us -> 0 us
  blocking collectives: 275 us -> 0 us
  Pallas kernels: 0 us -> 103 us
  starting transfers between devices: 38.8 us -> 0 us
  local copies, waits for them, and re-layouts: 42.2 us -> 5.53 us
  matrix products: 34.7 us -> 0 us
  other arithmetic: 26.9 us -> 0 us
  between operations: 15.7 us -> 0.65 us
    unnamed x2 -> x0, waiting for transfers between devices: 632 us -> none
    all_gather x1 -> x0, blocking collectives: 213 us -> none  [on_device(): lax.all_gather(adapter_down, ('sp', 'dp'), axis=0, tiled=True)]
    pallas_call x0 -> x1, Pallas kernels: none -> 103 us  [on_device(): pl.pallas_call(kernel, out_shape=(jax.ShapeDtypeStruct((CH, ROWS), F32),...]
    all_to_all x7 -> x0, waiting for transfers between devices: 84.7 us -> none  [the longest x1 24.6 us: on_device(): lax.all_to_all(head_major, 'sp', split_axis=0, concat_axis=1, tiled=True)]
    psum x1 -> x0, blocking collectives: 62.2 us -> none  [learner_step(): log_gains = lax.psum(partial_gain, ('sp', 'dp'))]
    all_to_all x7 -> x0, starting transfers between devices: 38.8 us -> none  [the longest x1 9.87 us: on_device(): lax.all_to_all(slots_wide(row_info).astype(jnp.bfloat16), 'dp', split_axi...]
    dot_general x14 -> x0, matrix products: 34.7 us -> none  [the longest x4 14.5 us: one_block(): jnp.dot(weights.astype(jnp.bfloat16), value_head, preferred_element_type=...]
    reduce_sum x9 -> x0, other arithmetic: 15 us -> none  [the longest x4 11.4 us: one_block(): totals = jnp.sum(weights, axis=1, keepdims=True)]
  transfers between devices with their start and end apart: 8 -> 0, of which waited for: 6 -> 0; matrix products, arithmetic and copies ran while one was open for 3% -> 0% of each run, Pallas kernels for 0% -> 0%
where the time goes in v1:
time: 110 us; the launch traced here: 109 us
  Pallas kernels  103 us (94%)
  local copies, waits for them, and re-layouts  5.53 us (5%)
    pallas_call x1, Pallas kernels, on_device(): pl.pallas_call(kernel, out_shape=(jax.ShapeDtypeStruct((CH, ROWS), F32),...  103 us
    unnamed x3, local copies, waits for them, and re-layouts  4.35 us

profile of v1, /device:TPU:1, one launch (start us, length us, event | category | flops | bytes accessed | tf_op | source)
XLA Modules:
  0.0 109.4 jit_solution(4071824732034032863)
XLA Ops:
  0.6 103.2 %policy_step.1 = (f32[64,256]{1,0:T(8,128)}, f32[64,512]{1,0:T(8,128)}, f32[8,128]{1,0:T(8,128)}, f32[24,128]{1,0:T(8,128)}) custom-call(bf16[1,256,3072]{2,1,0:T(8,128)(2,1)} %q_hbm.1, bf16[1,256,3072]{2,1,0:T(8,128)(2,1)} %k_hbm.1, bf16[1,256,3072]{2,1,0:T(8,128)(2,1)} %v_hbm.1, f32[64,256]{1,0:T(8,128)} %bitcast.20, f32[64,256]{1,0:T(8,128)} %bitcast.21, ...), custom_call_target="tpu_custom_call" | custom-call | flops 7000000000 | bytes 6000000 | tf_op jit(solution)/shard_map/policy_step/pallas_call | solution.py:416
  103.8 1.2 %slice_bitcast_fusion = f32[16]{0:T(128)} fusion(f32[8,128]{1,0:T(8,128)} %get-tuple-element.10), kind=kLoop, calls=%fused_computation | loop fusion | bytes 128 | tf_op jit(solution)/shard_map/squeeze | solution.py:468
  105.0 1.5 %copy.19 = f32[1,256,64]{1,2,0:T(8,128)} copy(f32[1,256,64]{1,2,0:T(8,128)} %bitcast.18) | data formatting | bytes 131072
  106.5 1.6 %copy.20 = f32[1,1,512,64]{2,3,1,0:T(8,128)} copy(f32[1,1,512,64]{2,3,1,0:T(8,128)} %bitcast.17) | data formatting | bytes 262144
  108.1 1.3 %copy.21 = f32[24,128]{1,0:T(8,128)} copy(f32[24,128]{1,0:T(8,128)} %get-tuple-element.19) | data formatting | bytes 24576

commit v2 on v1

--- a/solution.py
+++ b/solution.py
@@ -48,7 +48,7 @@
     q_hbm, k_hbm, v_hbm, lat_hbm, noise_hbm, hw_hbm, ad_ref, up_ref, adv_ref, len_ref, time_ref, dest_ref,
     next_ref, learn_ref, ratio_ref, grad_ref,
     qland, kland, vland, att, lat, noise, wt, hw, piece, wg, cs_out, cs_in, csb, hwb,
-    r1s, r1r, r2, slots, learn_in, g_out, g_in,
+    held, r1s, r1r, r2, slots, learn_in, g_out, g_in,
     loc_sem, s0, r0, sa, ra, sc, rc, s1, r1, s2, rr2, sl, rl, s3, r3,
 ):
     me = lax.axis_index("sp")
@@ -158,34 +158,7 @@
     wg[own_rows, :] = piece[...]
     for h in range(HEADS):
         vland[h, :, HD:] = jnp.ones((SEQ, HD), BF16)
-    hw_copy.wait()
-    for c in gather:
-        c.wait()
-    wt[0:CH, :] = hw[...]
-    wt[CH:, :] = jnp.transpose(wg[...])[CH:, :].astype(BF16)
     ones = jnp.ones((16, FEAT), BF16)
-    cs_out[...] = nt(ones, wt[...])[0:8]
-    cs_copies = [
-        pltpu.make_async_remote_copy(
-            src_ref=cs_out,
-            dst_ref=cs_in.at[i],
-            send_sem=sc.at[i],
-            recv_sem=rc.at[i],
-            device_id=(peer(i), vid),
-            device_id_type=MESH,
-        )
-        for i in range(NP)
-    ]
-    for c in cs_copies:
-        c.start()
-    cs_in[NP] = cs_out[...]
-    for c in cs_copies:
-        c.wait()
-    for i in range(NP + 1):
-        spread = jnp.transpose(jnp.broadcast_to(cs_in[i][0:1], (HD, HD)))
-        csb[i] = spread[CH:]
-        if i == NP:
-            hwb[...] = spread[:CH]
 
     length = len_ref[vid]
     moment = time_ref[vid].astype(F32)
@@ -198,8 +171,10 @@
     key_at = SEQ // 2 + lax.broadcasted_iota(jnp.int32, (1, SEQ // 2), 1)
     cap = jnp.where(key_at < length, 3e38, -1e30).astype(F32)
 
-    def attend(h, rows):
-        scores = nt(qland[h, rows, :], kland[h]) * (LOG2E * HD**-0.5)
+    def score(h, rows):
+        return nt(qland[h, rows, :], kland[h]) * (LOG2E * HD**-0.5)
+
+    def attend(h, rows, scores):
         first = scores[:, : SEQ // 2]
         second = jnp.minimum(scores[:, SEQ // 2 :], cap)
         highest = jnp.maximum(
@@ -211,19 +186,57 @@
         att[rows, h * HD : (h + 1) * HD] = (mixed[:, :HD] / mixed[:, HD:]).astype(BF16)
 
     def attend_all(h):
-        @pl.loop(0, NSP)
-        def _(b):
-            attend(h, rows_of(b))
-
-    for c in local + [lat_copy, noise_copy]:
-        c.wait()
-    for h in range(2):
-        for t in range(3):
-            n = h * 3 + t
-            sent(n)
-            issue(n + 3)
-            arrived(n)
-        attend_all(h)
+        held[0] = score(h, rows_of(0))
+
+        @pl.loop(0, NSP // 2)
+        def _(pair):
+            for half in range(2):
+                b = 2 * pair + half
+                held[1 - half] = score(h, rows_of((b + 1) % NSP))
+                attend(h, rows_of(b), held[half])
+
+    for c in local + [lat_copy, noise_copy, hw_copy]:
+        c.wait()
+    for n in range(3):
+        sent(n)
+        issue(n + 3)
+    for n in range(3):
+        arrived(n)
+    attend_all(0)
+
+    for c in gather:
+        c.wait()
+    wt[0:CH, :] = hw[...]
+    wt[CH:, :] = jnp.transpose(wg[...])[CH:, :].astype(BF16)
+    cs_out[...] = nt(ones, wt[...])[0:8]
+    cs_copies = [
+        pltpu.make_async_remote_copy(
+            src_ref=cs_out,
+            dst_ref=cs_in.at[i],
+            send_sem=sc.at[i],
+            recv_sem=rc.at[i],
+            device_id=(peer(i), vid),
+            device_id_type=MESH,
+        )
+        for i in range(NP)
+    ]
+    for c in cs_copies:
+        c.start()
+    cs_in[NP] = cs_out[...]
+    for n in range(3, 6):
+        sent(n)
+        issue(n + 3)
+    for n in range(3, 6):
+        arrived(n)
+    attend_all(1)
+
+    for c in cs_copies:
+        c.wait()
+    for i in range(NP + 1):
+        spread = jnp.transpose(jnp.broadcast_to(cs_in[i][0:1], (HD, HD)))
+        csb[i] = spread[CH:]
+        if i == NP:
+            hwb[...] = spread[:CH]
 
     for n in (6, 7):
         arrived(n)
@@ -259,14 +272,20 @@
         for i in range(NP)
     ]
     opposite = [OFFSETS.index(((4 - dx) % 4, (2 - dy) % 2)) for dx, dy in OFFSETS]
-    for i in range(NP):
-        groups[8][opposite[i]].wait_recv()
-        rows = rows_of(peer(i))
-        attend(2, rows)
-        r1s[i] = partial_sums(rows)
-        part_copies[i].start()
-    attend(2, rows_of(me))
-    r1r[NP] = partial_sums(rows_of(me))
+    turn = [rows_of(me)] + [rows_of(peer(i)) for i in range(NP)]
+    held[0] = score(2, turn[0])
+    for n in range(NSP + 1):
+        if n < NP:
+            groups[8][opposite[n]].wait_recv()
+        if n + 1 < NSP:
+            held[(n + 1) % 2] = score(2, turn[n + 1])
+        if n < NSP:
+            attend(2, turn[n], held[n % 2])
+        if n == 1:
+            r1r[NP] = partial_sums(turn[0])
+        if n > 1:
+            r1s[n - 2] = partial_sums(turn[n - 1])
+            part_copies[n - 2].start()
     for n in (6, 7, 8):
         sent(n)
     for c in part_copies:
@@ -367,9 +386,12 @@
     grad_rest = (grad - grad_high.astype(F32)).astype(BF16)
     product = tn(jnp.concatenate([grad_high, grad_rest], axis=0), jnp.concatenate([up, up], axis=0))
     product = product * pull[0:1]
+    high = log_gain.astype(BF16).astype(F32)
+    middle = (log_gain - high).astype(BF16).astype(F32)
+    line = lax.broadcasted_iota(jnp.int32, (8, HD), 0)
+    gain_rows = jnp.where(line == 0, high, jnp.where(line == 1, middle, jnp.where(line == 2, log_gain - high - middle, 0.0)))
     for k in range(NDP):
-        g_out[k, 0:OWN] = product[k * OWN : (k + 1) * OWN]
-        g_out[k, OWN : OWN + 8] = log_gain
+        g_out[k] = jnp.concatenate([product[k * OWN : (k + 1) * OWN], gain_rows], axis=0).astype(BF16)
     grad_copies = [
         pltpu.make_async_remote_copy(
             src_ref=g_out.at[dp_peer(e)],
@@ -394,15 +416,28 @@
 
     for c in grad_copies:
         c.wait()
-    summed = g_in[0, 0:OWN]
+    summed = g_in[0].astype(F32)
+    column = lax.broadcasted_iota(jnp.int32, (8, HD), 1)
+    gains = jnp.where(column == 0, summed[OWN:], 0.0)
     for k in range(1, NDP):
-        summed = summed + g_in[k, 0:OWN]
-    grad_ref[...] = summed
-    column = lax.broadcasted_iota(jnp.int32, (8, HD), 1)
-    gains = jnp.zeros((8, HD), F32)
-    for k in range(NDP):
-        gains = jnp.where(column == k, g_in[k, OWN : OWN + 8], gains)
-    ratio_ref[...] = jnp.exp(gains)
+        block = g_in[k].astype(F32)
+        summed = summed + block
+        gains = jnp.where(column == k, block[OWN:], gains)
+    grad_ref[...] = summed[:OWN]
+    ratio_ref[...] = jnp.exp(jnp.broadcast_to(gains[0:1] + gains[1:2] + gains[2:3], (8, HD)))
+
+
+def hand_over(next_in, learn_in, ratio_in, grad_in, next_out, learn_out, ratio_out, grad_out, sem):
+    copies = [
+        pltpu.make_async_copy(next_in, next_out, sem.at[0]),
+        pltpu.make_async_copy(learn_in, learn_out, sem.at[1]),
+        pltpu.make_async_copy(grad_in, grad_out, sem.at[2]),
+    ]
+    for c in copies:
+        c.start()
+    ratio_out[...] = ratio_in[0, :NDP]
+    for c in copies:
+        c.wait()
 
 
 def on_device(
@@ -438,13 +473,14 @@
             pltpu.VMEM((NSP, 8, HD), F32),
             pltpu.VMEM((NSP, CH, HD), F32),
             pltpu.VMEM((CH, HD), F32),
+            pltpu.VMEM((2, ROWS, SEQ), F32),
             pltpu.VMEM((NP, 144, ROWS), BF16),
             pltpu.VMEM((NSP, 144, ROWS), BF16),
             pltpu.VMEM((NSP, CH + 16, ROWS), BF16),
             pltpu.VMEM((512, HD), BF16),
             pltpu.VMEM((512, HD), BF16),
-            pltpu.VMEM((NDP, OWN + 8, HD), F32),
-            pltpu.VMEM((NDP, OWN + 8, HD), F32),
+            pltpu.VMEM((NDP, OWN + 8, HD), BF16),
+            pltpu.VMEM((NDP, OWN + 8, HD), BF16),
             dma((12,)),
             dma((9, NP)), dma((9, NP)),
             dma((NDP,)), dma((NDP,)),
@@ -455,7 +491,7 @@
             dma((NDP,)), dma((NDP,)),
         ],
         compiler_params=pltpu.CompilerParams(
-            collective_id=0, has_side_effects=True, vmem_limit_bytes=56 * 2**20
+            collective_id=0, has_side_effects=True, vmem_limit_bytes=60 * 2**20
         ),
         cost_estimate=pl.CostEstimate(
             flops=7 * 10**9, bytes_accessed=6 * 10**6, transcendentals=13 * 10**6
@@ -465,7 +501,20 @@
         queries, keys, values, latents[0].T, noise[0].T, head_weight.T, adapter_down, adapter_up.T, advantages,
         lengths, timesteps, destinations.reshape(1, 16),
     )
-    return nxt.T[None], learn.T[None, None], ratio[0, :NDP], grad
+    nxt, learn, ratio, grad = pl.pallas_call(
+        hand_over,
+        out_shape=(
+            jax.ShapeDtypeStruct((CH, ROWS), F32),
+            jax.ShapeDtypeStruct((CH, 512), F32),
+            jax.ShapeDtypeStruct((NDP,), F32),
+            jax.ShapeDtypeStruct((OWN, HD), F32),
+        ),
+        in_specs=[hbm, hbm, vmem, hbm],
+        out_specs=(hbm, hbm, vmem, hbm),
+        scratch_shapes=[dma((3,))],
+        name="hand_over",
+    )(nxt, learn, ratio, grad)
+    return nxt.T[None], learn.T[None, None], ratio, grad
 
 
 def solution(mesh):

time: 110 us -> 103 us (0.936)
  local copies, waits for them, and re-layouts: 5.53 us -> 0 us
    pallas_call x1, Pallas kernels: 103 us -> 93.2 us  [on_device(): pl.pallas_call(kernel, out_shape=(jax.ShapeDtypeStruct((CH, ROWS), F32),...]
    pallas_call x0 -> x1, Pallas kernels: none -> 8.65 us  [on_device(): pl.pallas_call(hand_over, out_shape=(jax.ShapeDtypeStruct((CH, ROWS), F32...]
    unnamed x3 -> x0, local copies, waits for them, and re-layouts: 4.35 us -> none
    squeeze x1 -> x0, local copies, waits for them, and re-layouts: 1.19 us -> none  [on_device(): return (nxt.T[None], learn.T[None, None], ratio[0, :NDP], grad)]
where the time goes in v2:
time: 103 us
  Pallas kernels  102 us (99%)
    pallas_call x1, Pallas kernels, on_device(): pl.pallas_call(kernel, out_shape=(jax.ShapeDtypeStruct((CH, ROWS), F32),...  93.2 us
    pallas_call x1, Pallas kernels, on_device(): pl.pallas_call(hand_over, out_shape=(jax.ShapeDtypeStruct((CH, ROWS), F32...  8.65 us

profile of v2, /device:TPU:1, one launch (start us, length us, event | category | flops | bytes accessed | tf_op | source)
XLA Modules:
  0.0 102.7 jit_solution(17504291564810202887)
XLA Ops:
  0.6 93.2 %policy_step.1 = (f32[64,256]{1,0:T(8,128)}, f32[64,512]{1,0:T(8,128)}, f32[8,128]{1,0:T(8,128)}, f32[24,128]{1,0:T(8,128)}) custom-call(bf16[1,256,3072]{2,1,0:T(8,128)(2,1)} %q_hbm.1, bf16[1,256,3072]{2,1,0:T(8,128)(2,1)} %k_hbm.1, bf16[1,256,3072]{2,1,0:T(8,128)(2,1)} %v_hbm.1, f32[64,256]{1,0:T(8,128)} %bitcast.17, f32[64,256]{1,0:T(8,128)} %bitcast.18, ...), custom_call_target="tpu_custom_call" | custom-call | flops 7000000000 | bytes 6000000 | tf_op jit(solution)/shard_map/policy_step/pallas_call | solution.py:451
  93.9 8.6 %hand_over.1 = (f32[64,256]{1,0:T(8,128)}, f32[64,512]{1,0:T(8,128)}, f32[16]{0:T(128)}, f32[24,128]{1,0:T(8,128)}) custom-call(f32[64,256]{1,0:T(8,128)} %get-tuple-element.12.next_in, f32[64,512]{1,0:T(8,128)} %get-tuple-element.13.learn_in, f32[8,128]{1,0:T(8,128)} %get-tuple-element.14.ratio_in, f32[24,128]{1,0:T(8,128)} %get-tuple-element.15.grad_in), custom_call_target="tpu_custom_call" | custom-call | tf_op jit(solution)/shard_map/hand_over/pallas_call | solution.py:504

commit v3 on v2

--- a/solution.py
+++ b/solution.py
@@ -45,10 +45,12 @@
 
 
 def kernel(
-    q_hbm, k_hbm, v_hbm, lat_hbm, noise_hbm, hw_hbm, ad_ref, up_ref, adv_ref, len_ref, time_ref, dest_ref,
+    q_hbm, k_hbm, v_hbm, lat_hbm, noise_hbm, hw_hbm, ad_ref, up_hbm, adv_hbm, len_hbm, time_hbm, dest_hbm,
+    next_hbm, learn_hbm, ratio_hbm, grad_hbm,
+    qland, kland, vland, att, prob, held, lat, noise, hw, up_ref, adv_ref, len_ref, time_ref, dest_ref,
     next_ref, learn_ref, ratio_ref, grad_ref,
-    qland, kland, vland, att, lat, noise, wt, hw, piece, wg, cs_out, cs_in, csb, hwb,
-    held, r1s, r1r, r2, slots, learn_in, g_out, g_in,
+    weight, early, stat, piece, wg, cs_out, cs_in, csb, offs, placing,
+    r1s, r1r, r2, slots, learn_in, g_out, g_in,
     loc_sem, s0, r0, sa, ra, sc, rc, s1, r1, s2, rr2, sl, rl, s3, r3,
 ):
     me = lax.axis_index("sp")
@@ -97,13 +99,26 @@
     hw_copy = pltpu.make_async_copy(
         hw_hbm.at[:, pl.ds(pl.multiple_of(me * FEAT, HD), FEAT)], hw, loc_sem.at[9]
     )
-    lat_copy = pltpu.make_async_copy(lat_hbm, lat, loc_sem.at[10])
-    noise_copy = pltpu.make_async_copy(noise_hbm, noise, loc_sem.at[11])
-    extra = [hw_copy, lat_copy, noise_copy]
+    small = [
+        pltpu.make_async_copy(src, dst, loc_sem.at[10 + n])
+        for n, (src, dst) in enumerate(
+            (
+                (up_hbm, up_ref),
+                (lat_hbm, lat),
+                (noise_hbm, noise),
+                (adv_hbm, adv_ref),
+                (len_hbm, len_ref),
+                (time_hbm, time_ref),
+                (dest_hbm, dest_ref),
+            )
+        )
+    ]
+    for c in small + [hw_copy]:
+        c.start()
 
     pl.semaphore_wait(barrier, NP + NDP - 1)
 
-    order = (0, 1, 2, 3, 4, 5, 6, 8, 7)
+    order = (0, 1, 2, 3, 4, 5, 7, 6, 8)
     groups = []
     for g in order:
         h, t = g // 3, g % 3
@@ -135,8 +150,10 @@
 
     for n in range(3):
         issue(n)
-    for c in local + extra:
-        c.start()
+    for c in local:
+        c.start()
+    for c in small:
+        c.wait()
 
     up = up_ref[...]
     up_low = jnp.concatenate([jnp.zeros_like(up), up], axis=0)
@@ -158,7 +175,6 @@
     wg[own_rows, :] = piece[...]
     for h in range(HEADS):
         vland[h, :, HD:] = jnp.ones((SEQ, HD), BF16)
-    ones = jnp.ones((16, FEAT), BF16)
 
     length = len_ref[vid]
     moment = time_ref[vid].astype(F32)
@@ -168,13 +184,24 @@
     live = jnp.where(token < length, 1.0, 0.0).astype(F32)
     row_weight = live / (jnp.full((1, ROWS), length.astype(F32), F32) * CH)
     gain = row_weight * inverse
+    offs[...] = noise_scale * noise[...]
+    lane = lax.broadcasted_iota(jnp.int32, (1, ROWS), 1)
+    targets = [dest_ref[0, b] for b in range(16)]
+    place = jnp.zeros((1, ROWS), jnp.int32)
+    for b in range(16):
+        rank = jnp.int32(0)
+        for a in range(b):
+            rank = rank + jnp.where(targets[a] == targets[b], 1, 0)
+        place = jnp.where(lane // 16 == b, targets[b] * 2 + rank, place)
+    place = place * 16 + lane % 16
+    placing[...] = (lax.broadcasted_iota(jnp.int32, (512, ROWS), 0) == place).astype(F32).astype(BF16)
     key_at = SEQ // 2 + lax.broadcasted_iota(jnp.int32, (1, SEQ // 2), 1)
     cap = jnp.where(key_at < length, 3e38, -1e30).astype(F32)
 
     def score(h, rows):
         return nt(qland[h, rows, :], kland[h]) * (LOG2E * HD**-0.5)
 
-    def attend(h, rows, scores):
+    def soften(scores):
         first = scores[:, : SEQ // 2]
         second = jnp.minimum(scores[:, SEQ // 2 :], cap)
         highest = jnp.maximum(
@@ -182,8 +209,32 @@
         )
         low = jnp.exp2(first - highest).astype(BF16)
         high = jnp.exp2(second - highest).astype(BF16)
-        mixed = nn(jnp.concatenate([low, high], axis=1), vland[h])
-        att[rows, h * HD : (h + 1) * HD] = (mixed[:, :HD] / mixed[:, HD:]).astype(BF16)
+        return jnp.concatenate([low, high], axis=1)
+
+    def finish(h, rows, mixed):
+        feature = (mixed[:, :HD] / mixed[:, HD:]).astype(BF16)
+        att[rows, h * HD : (h + 1) * HD] = feature
+        return feature
+
+    def moments(feature):
+        wide = feature.astype(F32)
+        average = jnp.sum(wide, axis=1, keepdims=True) * (1.0 / feature.shape[1])
+        centred = wide - average
+        return average, jnp.sum(centred * centred, axis=1, keepdims=True)
+
+    stat_lane = lax.broadcasted_iota(jnp.int32, (ROWS, HD), 1)
+
+    def block(h, rows, scores):
+        chances = soften(scores)
+        if h == 2:
+            prob[rows, :] = chances
+            return
+        finish(h, rows, nn(chances, vland[h]))
+        if h == 1:
+            feature = att[rows, 0 : 2 * HD]
+            early[rows, :] = nn(feature, weight[0 : 2 * HD, :])
+            average, square = moments(feature)
+            stat[rows, :] = jnp.where(stat_lane == 0, average, jnp.where(stat_lane == 1, square, 0.0))
 
     def attend_all(h):
         held[0] = score(h, rows_of(0))
@@ -193,9 +244,9 @@
             for half in range(2):
                 b = 2 * pair + half
                 held[1 - half] = score(h, rows_of((b + 1) % NSP))
-                attend(h, rows_of(b), held[half])
-
-    for c in local + [lat_copy, noise_copy, hw_copy]:
+                block(h, rows_of(b), held[half])
+
+    for c in local + [hw_copy]:
         c.wait()
     for n in range(3):
         sent(n)
@@ -206,9 +257,9 @@
 
     for c in gather:
         c.wait()
-    wt[0:CH, :] = hw[...]
-    wt[CH:, :] = jnp.transpose(wg[...])[CH:, :].astype(BF16)
-    cs_out[...] = nt(ones, wt[...])[0:8]
+    wide_head = jnp.concatenate([hw[...].astype(F32), jnp.zeros((CH, FEAT), F32)], axis=0)
+    weight[...] = (jnp.transpose(wide_head) + wg[...]).astype(BF16)
+    cs_out[...] = nn(jnp.ones((16, FEAT), BF16), weight[...])[0:8]
     cs_copies = [
         pltpu.make_async_remote_copy(
             src_ref=cs_out,
@@ -234,31 +285,29 @@
         c.wait()
     for i in range(NP + 1):
         spread = jnp.transpose(jnp.broadcast_to(cs_in[i][0:1], (HD, HD)))
-        csb[i] = spread[CH:]
-        if i == NP:
-            hwb[...] = spread[:CH]
+        csb[i] = jnp.concatenate([spread[CH:], spread[CH:]], axis=1)
 
     for n in (6, 7):
         arrived(n)
-
-    def partial_sums(rows):
-        feature = att[rows, :]
-        wide = feature.astype(F32)
-        centred = wide - jnp.sum(wide, axis=1, keepdims=True) * (1.0 / FEAT)
-        sums = nt(wt[...], centred.astype(BF16))
-        mean = nt(ones, feature) * (1.0 / FEAT)
-        square = nt(ones, (centred * centred).astype(BF16))
-        spread = jnp.concatenate([hwb[...], hwb[...]], axis=1)
-        velocity = sums[:CH] + spread * mean[0:1]
+    attend_all(2)
+    arrived(8)
+
+    def partial_sums(rows, mixed):
+        feature = finish(2, rows, mixed)
+        sums = early[rows, :] + nn(feature, weight[2 * HD :, :])
+        average, square = moments(feature)
+        columns = stat[rows, :] + jnp.where(stat_lane == 2, average, jnp.where(stat_lane == 3, square, 0.0))
+        lines = jnp.transpose(columns)
+        apart = lines[0:1] - lines[2:3]
+        mean = lines[0:1] - apart * (1.0 / 3.0)
+        square = lines[1:2] + lines[3:4] + apart * apart * (2.0 * HD / 3.0)
+        sums = jnp.transpose(sums)
         line = lax.broadcasted_iota(jnp.int32, (16, ROWS), 0)
         mean_high = mean.astype(BF16).astype(F32)
         square_high = square.astype(BF16).astype(F32)
-        stats = jnp.where(
-            line == 0,
-            mean_high,
-            jnp.where(line == 1, mean - mean_high, jnp.where(line == 2, square_high, square - square_high)),
-        )
-        return jnp.concatenate([velocity, sums[CH:], stats], axis=0).astype(BF16)
+        stats = jnp.where(line == 0, mean_high, jnp.where(line == 1, mean - mean_high, 0.0))
+        stats = jnp.where(line == 2, square_high, jnp.where(line == 3, square - square_high, stats))
+        return jnp.concatenate([sums[:CH], sums[CH:] - csb[NP] * mean, stats], axis=0).astype(BF16)
 
     part_copies = [
         pltpu.make_async_remote_copy(
@@ -271,30 +320,23 @@
         )
         for i in range(NP)
     ]
-    opposite = [OFFSETS.index(((4 - dx) % 4, (2 - dy) % 2)) for dx, dy in OFFSETS]
-    turn = [rows_of(me)] + [rows_of(peer(i)) for i in range(NP)]
-    held[0] = score(2, turn[0])
-    for n in range(NSP + 1):
+    turn = [rows_of(peer(i)) for i in range(NP)] + [rows_of(me)]
+    mixed = nn(prob[turn[0], :], vland[2])
+    for n in range(NSP):
         if n < NP:
-            groups[8][opposite[n]].wait_recv()
-        if n + 1 < NSP:
-            held[(n + 1) % 2] = score(2, turn[n + 1])
-        if n < NSP:
-            attend(2, turn[n], held[n % 2])
-        if n == 1:
-            r1r[NP] = partial_sums(turn[0])
-        if n > 1:
-            r1s[n - 2] = partial_sums(turn[n - 1])
-            part_copies[n - 2].start()
+            following = nn(prob[turn[n + 1], :], vland[2])
+            r1s[n] = partial_sums(turn[n], mixed)
+            part_copies[n].start()
+            mixed = following
+        else:
+            r1r[NP] = partial_sums(turn[n], mixed)
     for n in (6, 7, 8):
         sent(n)
     for c in part_copies:
         c.wait()
 
     parts = [r1r[i].astype(F32) for i in range(NP + 1)]
-    total = parts[0][: 2 * CH]
-    for p in parts[1:]:
-        total = total + p[: 2 * CH]
+    total = functools.reduce(jnp.add, [p[: 2 * CH] for p in parts])
     means = [p[128:129] + p[129:130] for p in parts]
     squares = [p[130:131] + p[131:132] for p in parts]
     mean = functools.reduce(jnp.add, means) * (1.0 / NSP)
@@ -303,9 +345,9 @@
     rstd = lax.rsqrt(variance * (1.0 / (FEAT * NSP)) + NORM_EPS)
     inner = total[CH:]
     for i in range(NP + 1):
-        inner = inner + jnp.concatenate([csb[i], csb[i]], axis=1) * gaps[i]
+        inner = inner + csb[i] * gaps[i]
     delta = inner * rstd
-    offset = noise_scale * noise[...]
+    offset = offs[...]
     gap = offset - STEP * delta
     unit = (gap * (gain * (2.0 * STEP) * rstd)).astype(BF16)
     terms = gain * jnp.sum(offset * offset - gap * gap, axis=0, keepdims=True)
@@ -333,18 +375,8 @@
     for c in unit_copies:
         c.start()
 
-    lane = lax.broadcasted_iota(jnp.int32, (1, ROWS), 1)
-    targets = [dest_ref[0, b] for b in range(16)]
-    place = jnp.zeros((1, ROWS), jnp.int32)
-    for b in range(16):
-        rank = jnp.int32(0)
-        for a in range(b):
-            rank = rank + jnp.where(targets[a] == targets[b], 1, 0)
-        place = jnp.where(lane // 16 == b, targets[b] * 2 + rank, place)
-    place = place * 16 + lane % 16
-    placing = (lax.broadcasted_iota(jnp.int32, (512, ROWS), 0) == place).astype(F32).astype(BF16)
     delta_low = delta.astype(BF16)
-    slots[...] = nt(placing, jnp.concatenate([delta_low, jnp.zeros_like(delta_low)], axis=0)).astype(BF16)
+    slots[...] = nt(placing[...], jnp.concatenate([delta_low, jnp.zeros_like(delta_low)], axis=0)).astype(BF16)
     mine = pl.ds(pl.multiple_of(vid * 32, 32), 32)
     learn_copies = [
         pltpu.make_async_remote_copy(
@@ -361,6 +393,13 @@
         c.start()
     learn_in[mine, :] = slots[mine, :]
     next_ref[...] = (lat[...] - STEP * total[:CH]) + offset
+    outward = [
+        pltpu.make_async_copy(src, dst, loc_sem.at[18 + n])
+        for n, (src, dst) in enumerate(
+            ((next_ref, next_hbm), (learn_ref, learn_hbm), (ratio_ref, ratio_hbm), (grad_ref, grad_hbm))
+        )
+    ]
+    outward[0].start()
 
     def grad_part(s):
         u = r2[s, 0:CH]
@@ -411,6 +450,7 @@
         c.wait()
     select = lax.broadcasted_iota(jnp.int32, (CH, HD), 0) == lax.broadcasted_iota(jnp.int32, (CH, HD), 1)
     learn_ref[...] = nt(select.astype(F32).astype(BF16), learn_in[...])
+    outward[1].start()
     for c in unit_copies:
         c.wait_send()
 
@@ -424,20 +464,18 @@
         summed = summed + block
         gains = jnp.where(column == k, block[OWN:], gains)
     grad_ref[...] = summed[:OWN]
+    outward[3].start()
     ratio_ref[...] = jnp.exp(jnp.broadcast_to(gains[0:1] + gains[1:2] + gains[2:3], (8, HD)))
-
-
-def hand_over(next_in, learn_in, ratio_in, grad_in, next_out, learn_out, ratio_out, grad_out, sem):
-    copies = [
-        pltpu.make_async_copy(next_in, next_out, sem.at[0]),
-        pltpu.make_async_copy(learn_in, learn_out, sem.at[1]),
-        pltpu.make_async_copy(grad_in, grad_out, sem.at[2]),
-    ]
-    for c in copies:
-        c.start()
+    outward[2].start()
+    for c in outward:
+        c.wait()
+
+
+def hand_over(next_in, learn_in, ratio_in, grad_in, next_out, learn_out, ratio_out, grad_out):
+    next_out[...] = next_in[...]
+    learn_out[...] = learn_in[...]
+    grad_out[...] = grad_in[...]
     ratio_out[...] = ratio_in[0, :NDP]
-    for c in copies:
-        c.wait()
 
 
 def on_device(
@@ -446,7 +484,6 @@
 ):
     hbm = pl.BlockSpec(memory_space=pl.ANY)
     vmem = pl.BlockSpec(memory_space=pltpu.VMEM)
-    smem = pl.BlockSpec(memory_space=pltpu.SMEM)
     dma = pltpu.SemaphoreType.DMA
     nxt, learn, ratio, grad = pl.pallas_call(
         kernel,
@@ -456,24 +493,37 @@
             jax.ShapeDtypeStruct((8, HD), F32),
             jax.ShapeDtypeStruct((OWN, HD), F32),
         ),
-        in_specs=[hbm] * 6 + [vmem] * 2 + [smem] * 4,
-        out_specs=(vmem,) * 4,
+        in_specs=[hbm] * 6 + [vmem] + [hbm] * 5,
+        out_specs=(hbm,) * 4,
         scratch_shapes=[
             pltpu.VMEM((HEADS, SEQ, HD), BF16),
             pltpu.VMEM((HEADS, SEQ, HD), BF16),
             pltpu.VMEM((HEADS, SEQ, 2 * HD), BF16),
             pltpu.VMEM((SEQ, FEAT), BF16),
+            pltpu.VMEM((SEQ, SEQ), BF16),
+            pltpu.VMEM((2, ROWS, SEQ), F32),
             pltpu.VMEM((CH, ROWS), F32),
             pltpu.VMEM((CH, ROWS), F32),
-            pltpu.VMEM((2 * CH, FEAT), BF16),
             pltpu.VMEM((CH, FEAT), BF16),
+            pltpu.VMEM((CH, HD), BF16),
+            pltpu.SMEM((NDP,), F32),
+            pltpu.SMEM((NDP,), jnp.int32),
+            pltpu.SMEM((NDP,), jnp.int32),
+            pltpu.SMEM((1, 16), jnp.int32),
+            pltpu.VMEM((CH, ROWS), F32),
+            pltpu.VMEM((CH, 512), F32),
+            pltpu.VMEM((8, HD), F32),
+            pltpu.VMEM((OWN, HD), F32),
+            pltpu.VMEM((FEAT, HD), BF16),
+            pltpu.VMEM((SEQ, HD), F32),
+            pltpu.VMEM((SEQ, HD), F32),
             pltpu.VMEM((OWN, HD), F32),
             pltpu.VMEM((FEAT, HD), F32),
             pltpu.VMEM((8, HD), F32),
             pltpu.VMEM((NSP, 8, HD), F32),
-            pltpu.VMEM((NSP, CH, HD), F32),
-            pltpu.VMEM((CH, HD), F32),
-            pltpu.VMEM((2, ROWS, SEQ), F32),
+            pltpu.VMEM((NSP, CH, ROWS), F32),
+            pltpu.VMEM((CH, ROWS), F32),
+            pltpu.VMEM((512, ROWS), BF16),
             pltpu.VMEM((NP, 144, ROWS), BF16),
             pltpu.VMEM((NSP, 144, ROWS), BF16),
             pltpu.VMEM((NSP, CH + 16, ROWS), BF16),
@@ -481,7 +531,7 @@
             pltpu.VMEM((512, HD), BF16),
             pltpu.VMEM((NDP, OWN + 8, HD), BF16),
             pltpu.VMEM((NDP, OWN + 8, HD), BF16),
-            dma((12,)),
+            dma((22,)),
             dma((9, NP)), dma((9, NP)),
             dma((NDP,)), dma((NDP,)),
             dma((NP,)), dma((NP,)),
@@ -509,9 +559,8 @@
             jax.ShapeDtypeStruct((NDP,), F32),
             jax.ShapeDtypeStruct((OWN, HD), F32),
         ),
-        in_specs=[hbm, hbm, vmem, hbm],
-        out_specs=(hbm, hbm, vmem, hbm),
-        scratch_shapes=[dma((3,))],
+        in_specs=[vmem] * 4,
+        out_specs=(vmem,) * 4,
         name="hand_over",
     )(nxt, learn, ratio, grad)
     return nxt.T[None], learn.T[None, None], ratio, grad

time: 103 us -> 98.2 us (0.953)
  Pallas kernels: 102 us -> 97.3 us
    pallas_call x1, Pallas kernels: 8.65 us -> 1.59 us  [on_device(): pl.pallas_call(hand_over, out_shape=(jax.ShapeDtypeStruct((CH, ROWS), F32...]
    pallas_call x1, Pallas kernels: 93.2 us -> 95.7 us  [on_device(): pl.pallas_call(kernel, out_shape=(jax.ShapeDtypeStruct((CH, ROWS), F32),...]
where the time goes in v3:
time: 98.2 us; the launch traced here: 98 us
  Pallas kernels  97.3 us (99%)
    pallas_call x1, Pallas kernels, on_device(): pl.pallas_call(kernel, out_shape=(jax.ShapeDtypeStruct((CH, ROWS), F32),...  95.7 us

profile of v3, /device:TPU:1, one launch (start us, length us, event | category | flops | bytes accessed | tf_op | source)
XLA Modules:
  0.0 98.0 jit_solution(17004958041843727055)
XLA Ops:
  0.6 95.7 %policy_step.1 = (f32[64,256]{1,0:T(8,128)}, f32[64,512]{1,0:T(8,128)}, f32[8,128]{1,0:T(8,128)}, f32[24,128]{1,0:T(8,128)}) custom-call(bf16[1,256,3072]{2,1,0:T(8,128)(2,1)} %q_hbm.1, bf16[1,256,3072]{2,1,0:T(8,128)(2,1)} %k_hbm.1, bf16[1,256,3072]{2,1,0:T(8,128)(2,1)} %v_hbm.1, f32[64,256]{1,0:T(8,128)} %bitcast.17, f32[64,256]{1,0:T(8,128)} %bitcast.18, ...), custom_call_target="tpu_custom_call" | custom-call | flops 7000000000 | bytes 6000000 | tf_op jit(solution)/shard_map/policy_step/pallas_call | solution.py:488
  96.4 1.6 %hand_over.1 = (f32[64,256]{1,0:T(8,128)}, f32[64,512]{1,0:T(8,128)}, f32[16]{0:T(128)}, f32[24,128]{1,0:T(8,128)}) custom-call(f32[64,256]{1,0:T(8,128)} %get-tuple-element.12.next_in, f32[64,512]{1,0:T(8,128)} %get-tuple-element.13.learn_in, f32[8,128]{1,0:T(8,128)} %get-tuple-element.14.ratio_in, f32[24,128]{1,0:T(8,128)} %get-tuple-element.15.grad_in), custom_call_target="tpu_custom_call" | custom-call | tf_op jit(solution)/shard_map/hand_over/pallas_call | solution.py:554

commit v4 on v3

--- a/solution.py
+++ b/solution.py
@@ -21,6 +21,7 @@
 NSP = 8
 NDP = 16
 ROWS = 256
+HALF = 128
 SEQ = 2048
 HEADS = 3
 FEAT = HEADS * HD
@@ -49,7 +50,7 @@
     next_hbm, learn_hbm, ratio_hbm, grad_hbm,
     qland, kland, vland, att, prob, held, lat, noise, hw, up_ref, adv_ref, len_ref, time_ref, dest_ref,
     next_ref, learn_ref, ratio_ref, grad_ref,
-    weight, early, stat, piece, wg, cs_out, cs_in, csb, offs, placing,
+    weight, early, early_square, piece, wg, cs_out, cs_in, csb, offs, placing,
     r1s, r1r, r2, slots, learn_in, g_out, g_in,
     loc_sem, s0, r0, sa, ra, sc, rc, s1, r1, s2, rr2, sl, rl, s3, r3,
 ):
@@ -216,15 +217,14 @@
         att[rows, h * HD : (h + 1) * HD] = feature
         return feature
 
-    def moments(feature):
+    def squares_of(feature):
         wide = feature.astype(F32)
         average = jnp.sum(wide, axis=1, keepdims=True) * (1.0 / feature.shape[1])
         centred = wide - average
-        return average, jnp.sum(centred * centred, axis=1, keepdims=True)
-
-    stat_lane = lax.broadcasted_iota(jnp.int32, (ROWS, HD), 1)
-
-    def block(h, rows, scores):
+        return nt(jnp.ones((16, feature.shape[1]), BF16), (centred * centred).astype(BF16))
+
+    def block(h, b, scores):
+        rows = rows_of(b)
         chances = soften(scores)
         if h == 2:
             prob[rows, :] = chances
@@ -232,9 +232,8 @@
         finish(h, rows, nn(chances, vland[h]))
         if h == 1:
             feature = att[rows, 0 : 2 * HD]
-            early[rows, :] = nn(feature, weight[0 : 2 * HD, :])
-            average, square = moments(feature)
-            stat[rows, :] = jnp.where(stat_lane == 0, average, jnp.where(stat_lane == 1, square, 0.0))
+            early[b] = nt(weight[:, 0 : 2 * HD], feature)
+            early_square[b] = squares_of(feature)[0:8]
 
     def attend_all(h):
         held[0] = score(h, rows_of(0))
@@ -244,7 +243,7 @@
             for half in range(2):
                 b = 2 * pair + half
                 held[1 - half] = score(h, rows_of((b + 1) % NSP))
-                block(h, rows_of(b), held[half])
+                block(h, b, held[half])
 
     for c in local + [hw_copy]:
         c.wait()
@@ -257,9 +256,10 @@
 
     for c in gather:
         c.wait()
-    wide_head = jnp.concatenate([hw[...].astype(F32), jnp.zeros((CH, FEAT), F32)], axis=0)
-    weight[...] = (jnp.transpose(wide_head) + wg[...]).astype(BF16)
-    cs_out[...] = nn(jnp.ones((16, FEAT), BF16), weight[...])[0:8]
+    weight[0:CH, :] = hw[...]
+    weight[CH : 2 * CH, :] = jnp.transpose(wg[...])[CH:, :].astype(BF16)
+    weight[2 * CH :, :] = jnp.ones((16, FEAT), BF16)
+    cs_out[...] = nt(jnp.ones((16, FEAT), BF16), weight[0 : 2 * CH, :])[0:8]
     cs_copies = [
         pltpu.make_async_remote_copy(
             src_ref=cs_out,
@@ -285,97 +285,123 @@
         c.wait()
     for i in range(NP + 1):
         spread = jnp.transpose(jnp.broadcast_to(cs_in[i][0:1], (HD, HD)))
-        csb[i] = jnp.concatenate([spread[CH:], spread[CH:]], axis=1)
+        csb[i] = spread[CH:]
 
     for n in (6, 7):
         arrived(n)
     attend_all(2)
     arrived(8)
 
-    def partial_sums(rows, mixed):
-        feature = finish(2, rows, mixed)
-        sums = early[rows, :] + nn(feature, weight[2 * HD :, :])
-        average, square = moments(feature)
-        columns = stat[rows, :] + jnp.where(stat_lane == 2, average, jnp.where(stat_lane == 3, square, 0.0))
-        lines = jnp.transpose(columns)
-        apart = lines[0:1] - lines[2:3]
-        mean = lines[0:1] - apart * (1.0 / 3.0)
-        square = lines[1:2] + lines[3:4] + apart * apart * (2.0 * HD / 3.0)
-        sums = jnp.transpose(sums)
-        line = lax.broadcasted_iota(jnp.int32, (16, ROWS), 0)
-        mean_high = mean.astype(BF16).astype(F32)
-        square_high = square.astype(BF16).astype(F32)
-        stats = jnp.where(line == 0, mean_high, jnp.where(line == 1, mean - mean_high, 0.0))
-        stats = jnp.where(line == 2, square_high, jnp.where(line == 3, square - square_high, stats))
-        return jnp.concatenate([sums[:CH], sums[CH:] - csb[NP] * mean, stats], axis=0).astype(BF16)
-
+    owners = [peer(i) for i in range(NP)] + [me]
     part_copies = [
-        pltpu.make_async_remote_copy(
-            src_ref=r1s.at[i],
-            dst_ref=r1r.at[i],
-            send_sem=s1.at[i],
-            recv_sem=r1.at[i],
-            device_id=(peer(i), vid),
-            device_id_type=MESH,
-        )
-        for i in range(NP)
+        [
+            pltpu.make_async_remote_copy(
+                src_ref=r1s.at[half, i],
+                dst_ref=r1r.at[half, i],
+                send_sem=s1.at[half, i],
+                recv_sem=r1.at[half, i],
+                device_id=(peer(i), vid),
+                device_id_type=MESH,
+            )
+            for i in range(NP)
+        ]
+        for half in range(2)
     ]
-    turn = [rows_of(peer(i)) for i in range(NP)] + [rows_of(me)]
-    mixed = nn(prob[turn[0], :], vland[2])
-    for n in range(NSP):
-        if n < NP:
-            following = nn(prob[turn[n + 1], :], vland[2])
-            r1s[n] = partial_sums(turn[n], mixed)
-            part_copies[n].start()
-            mixed = following
-        else:
-            r1r[NP] = partial_sums(turn[n], mixed)
+
+    def tokens_of(s, half):
+        return pl.ds(pl.multiple_of(s * ROWS + half * HALF, HALF), HALF)
+
+    def mix(half, pair):
+        chances = [prob[tokens_of(owners[2 * pair + one], half), :] for one in range(2)]
+        return nn(jnp.concatenate(chances, axis=0), vland[2])
+
+    row16 = lax.broadcasted_iota(jnp.int32, (16, HALF), 0)
+
+    def partial_sums(half, pair, mixed):
+        feature = (mixed[:, :HD] / mixed[:, HD:]).astype(BF16)
+        sums = nt(weight[:, 2 * HD :], feature)
+        late_square = squares_of(feature)
+        for one in range(2):
+            n = 2 * pair + one
+            part = slice(one * HALF, (one + 1) * HALF)
+            span = slice(half * HALF, (half + 1) * HALF)
+            att[tokens_of(owners[n], half), 2 * HD :] = feature[part, :]
+            before = early[owners[n], :, span]
+            late = sums[:, part]
+            whole = before + late
+            mean = whole[2 * CH : 2 * CH + 1] * (1.0 / FEAT)
+            apart = before[2 * CH : 2 * CH + 1] * (0.5 / HD) - late[2 * CH : 2 * CH + 1] * (1.0 / HD)
+            square = early_square[owners[n], 0:1, span] + late_square[0:1, part]
+            square = square + apart * apart * (2.0 * HD / 3.0)
+            mean_high = mean.astype(BF16).astype(F32)
+            square_high = square.astype(BF16).astype(F32)
+            stats = jnp.where(row16 == 0, mean_high, jnp.where(row16 == 1, mean - mean_high, 0.0))
+            stats = jnp.where(row16 == 2, square_high, jnp.where(row16 == 3, square - square_high, stats))
+            message = jnp.concatenate([whole[:CH], whole[CH : 2 * CH] - csb[NP] * mean, stats], axis=0).astype(BF16)
+            if n < NP:
+                r1s[half, n] = message
+                part_copies[half][n].start()
+            else:
+                r1r[half, NP] = message
+
+    steps = [(half, pair) for half in range(2) for pair in range(NSP // 2)]
+    mixed = mix(*steps[0])
+    for n, step in enumerate(steps):
+        following = mix(*steps[n + 1]) if n + 1 < len(steps) else None
+        partial_sums(*step, mixed)
+        mixed = following
     for n in (6, 7, 8):
         sent(n)
-    for c in part_copies:
-        c.wait()
-
-    parts = [r1r[i].astype(F32) for i in range(NP + 1)]
-    total = functools.reduce(jnp.add, [p[: 2 * CH] for p in parts])
-    means = [p[128:129] + p[129:130] for p in parts]
-    squares = [p[130:131] + p[131:132] for p in parts]
-    mean = functools.reduce(jnp.add, means) * (1.0 / NSP)
-    gaps = [m - mean for m in means]
-    variance = functools.reduce(jnp.add, squares) + FEAT * functools.reduce(jnp.add, [g * g for g in gaps])
-    rstd = lax.rsqrt(variance * (1.0 / (FEAT * NSP)) + NORM_EPS)
-    inner = total[CH:]
-    for i in range(NP + 1):
-        inner = inner + csb[i] * gaps[i]
-    delta = inner * rstd
-    offset = offs[...]
-    gap = offset - STEP * delta
-    unit = (gap * (gain * (2.0 * STEP) * rstd)).astype(BF16)
-    terms = gain * jnp.sum(offset * offset - gap * gap, axis=0, keepdims=True)
-    line = lax.broadcasted_iota(jnp.int32, (16, ROWS), 0)
-    mean_high = mean.astype(BF16).astype(F32)
-    terms_high = terms.astype(BF16).astype(F32)
-    terms_rest = terms - terms_high
-    terms_mid = terms_rest.astype(BF16).astype(F32)
-    side = jnp.where(line == 0, mean_high, jnp.where(line == 1, mean - mean_high, 0.0))
-    side = jnp.where(line == 2, terms_high, side)
-    side = jnp.where(line == 3, terms_mid, jnp.where(line == 4, terms_rest - terms_mid, side))
-    r2[me, 0:CH] = unit
-    r2[me, CH : CH + 16] = side.astype(BF16)
-    unit_copies = [
-        pltpu.make_async_remote_copy(
-            src_ref=r2.at[me],
-            dst_ref=r2.at[me],
-            send_sem=s2.at[i],
-            recv_sem=rr2.at[i],
-            device_id=(peer(i), vid),
-            device_id_type=MESH,
-        )
-        for i in range(NP)
-    ]
-    for c in unit_copies:
-        c.start()
-
-    delta_low = delta.astype(BF16)
+
+    def own_tokens(half):
+        for c in part_copies[half]:
+            c.wait_recv()
+        span = slice(half * HALF, (half + 1) * HALF)
+        parts = [r1r[half, i].astype(F32) for i in range(NP + 1)]
+        total = functools.reduce(jnp.add, [p[: 2 * CH] for p in parts])
+        means = [p[128:129] + p[129:130] for p in parts]
+        squares = [p[130:131] + p[131:132] for p in parts]
+        mean = functools.reduce(jnp.add, means) * (1.0 / NSP)
+        gaps = [m - mean for m in means]
+        variance = functools.reduce(jnp.add, squares) + FEAT * functools.reduce(jnp.add, [g * g for g in gaps])
+        rstd = lax.rsqrt(variance * (1.0 / (FEAT * NSP)) + NORM_EPS)
+        inner = total[CH:]
+        for i in range(NP + 1):
+            inner = inner + csb[i] * gaps[i]
+        delta = inner * rstd
+        offset = offs[:, span]
+        gap = offset - STEP * delta
+        unit = (gap * (gain[:, span] * (2.0 * STEP) * rstd)).astype(BF16)
+        terms = gain[:, span] * jnp.sum(offset * offset - gap * gap, axis=0, keepdims=True)
+        mean_high = mean.astype(BF16).astype(F32)
+        terms_high = terms.astype(BF16).astype(F32)
+        terms_rest = terms - terms_high
+        terms_mid = terms_rest.astype(BF16).astype(F32)
+        side = jnp.where(row16 == 0, mean_high, jnp.where(row16 == 1, mean - mean_high, 0.0))
+        side = jnp.where(row16 == 2, terms_high, side)
+        side = jnp.where(row16 == 3, terms_mid, jnp.where(row16 == 4, terms_rest - terms_mid, side))
+        r2[half, me] = jnp.concatenate([unit.astype(F32), side], axis=0).astype(BF16)
+        copies = [
+            pltpu.make_async_remote_copy(
+                src_ref=r2.at[half, me],
+                dst_ref=r2.at[half, me],
+                send_sem=s2.at[half, i],
+                recv_sem=rr2.at[half, i],
+                device_id=(peer(i), vid),
+                device_id_type=MESH,
+            )
+            for i in range(NP)
+        ]
+        for c in copies:
+            c.start()
+        next_ref[:, span] = (lat[:, span] - STEP * total[:CH]) + offset
+        return delta.astype(BF16), copies
+
+    delta_first, copies_first = own_tokens(0)
+    delta_second, copies_second = own_tokens(1)
+    unit_copies = [copies_first, copies_second]
+
+    delta_low = jnp.concatenate([delta_first, delta_second], axis=1)
     slots[...] = nt(placing[...], jnp.concatenate([delta_low, jnp.zeros_like(delta_low)], axis=0)).astype(BF16)
     mine = pl.ds(pl.multiple_of(vid * 32, 32), 32)
     learn_copies = [
@@ -392,7 +418,6 @@
     for c in learn_copies:
         c.start()
     learn_in[mine, :] = slots[mine, :]
-    next_ref[...] = (lat[...] - STEP * total[:CH]) + offset
     outward = [
         pltpu.make_async_copy(src, dst, loc_sem.at[18 + n])
         for n, (src, dst) in enumerate(
@@ -401,19 +426,20 @@
     ]
     outward[0].start()
 
-    def grad_part(s):
-        u = r2[s, 0:CH]
-        side = r2[s, CH : CH + 16]
-        shift = nt(u, side)
-        return nn(u, att[rows_of(s), :]) - (shift[:, 0:1] + shift[:, 1:2])
-
-    grad = grad_part(me)
-    for i in range(NP):
-        unit_copies[i].wait_recv()
-        grad = grad + grad_part(source(i))
-    sides = r2[0, CH : CH + 16].astype(F32)
+    def grad_part(half, s):
+        u = r2[half, s, 0:CH]
+        shift = nt(u, r2[half, s, CH : CH + 16])
+        return nn(u, att[tokens_of(s, half), :]) - (shift[:, 0:1] + shift[:, 1:2])
+
+    grad = grad_part(0, me) + grad_part(1, me)
+    for half in range(2):
+        for i in range(NP):
+            unit_copies[half][i].wait_recv()
+        for i in range(NP):
+            grad = grad + grad_part(half, source(i))
+    sides = r2[0, 0, CH : CH + 16].astype(F32) + r2[1, 0, CH : CH + 16].astype(F32)
     for s in range(1, NSP):
-        sides = sides + r2[s, CH : CH + 16].astype(F32)
+        sides = sides + r2[0, s, CH : CH + 16].astype(F32) + r2[1, s, CH : CH + 16].astype(F32)
     log_gain = jnp.sum(sides[2:3] + sides[3:4] + sides[4:5], axis=1, keepdims=True)
     log_gain = jnp.broadcast_to(log_gain, (8, HD))
     ratio = jnp.exp(log_gain)
@@ -451,7 +477,7 @@
     select = lax.broadcasted_iota(jnp.int32, (CH, HD), 0) == lax.broadcasted_iota(jnp.int32, (CH, HD), 1)
     learn_ref[...] = nt(select.astype(F32).astype(BF16), learn_in[...])
     outward[1].start()
-    for c in unit_copies:
+    for c in unit_copies[0] + unit_copies[1] + part_copies[0] + part_copies[1]:
         c.wait_send()
 
     for c in grad_copies:
@@ -514,19 +540,19 @@
             pltpu.VMEM((CH, 512), F32),
             pltpu.VMEM((8, HD), F32),
             pltpu.VMEM((OWN, HD), F32),
-            pltpu.VMEM((FEAT, HD), BF16),
-            pltpu.VMEM((SEQ, HD), F32),
-            pltpu.VMEM((SEQ, HD), F32),
+            pltpu.VMEM((144, FEAT), BF16),
+            pltpu.VMEM((NSP, 144, ROWS), F32),
+            pltpu.VMEM((NSP, 8, ROWS), F32),
             pltpu.VMEM((OWN, HD), F32),
             pltpu.VMEM((FEAT, HD), F32),
             pltpu.VMEM((8, HD), F32),
             pltpu.VMEM((NSP, 8, HD), F32),
-            pltpu.VMEM((NSP, CH, ROWS), F32),
+            pltpu.VMEM((NSP, CH, HD), F32),
             pltpu.VMEM((CH, ROWS), F32),
             pltpu.VMEM((512, ROWS), BF16),
-            pltpu.VMEM((NP, 144, ROWS), BF16),
-            pltpu.VMEM((NSP, 144, ROWS), BF16),
-            pltpu.VMEM((NSP, CH + 16, ROWS), BF16),
+            pltpu.VMEM((2, NP, 144, HALF), BF16),
+            pltpu.VMEM((2, NSP, 144, HALF), BF16),
+            pltpu.VMEM((2, NSP, CH + 16, HALF), BF16),
             pltpu.VMEM((512, HD), BF16),
             pltpu.VMEM((512, HD), BF16),
             pltpu.VMEM((NDP, OWN + 8, HD), BF16),
@@ -535,8 +561,8 @@
             dma((9, NP)), dma((9, NP)),
             dma((NDP,)), dma((NDP,)),
             dma((NP,)), dma((NP,)),
-            dma((NP,)), dma((NP,)),
-            dma((NP,)), dma((NP,)),
+            dma((2, NP)), dma((2, NP)),
+            dma((2, NP)), dma((2, NP)),
             dma((NDP,)), dma((NDP,)),
             dma((NDP,)), dma((NDP,)),
         ],

time: 98.2 us -> 96.8 us (0.986)
  Pallas kernels: 97.3 us -> 95.9 us
    pallas_call x1, Pallas kernels: 95.7 us -> 94.3 us  [on_device(): pl.pallas_call(kernel, out_shape=(jax.ShapeDtypeStruct((CH, ROWS), F32),...]
where the time goes in v4:
time: 96.8 us; the launch traced here: 96.6 us
  Pallas kernels  95.9 us (99%)
    pallas_call x1, Pallas kernels, on_device(): pl.pallas_call(kernel, out_shape=(jax.ShapeDtypeStruct((CH, ROWS), F32),...  94.3 us

profile of v4, /device:TPU:1, one launch (start us, length us, event | category | flops | bytes accessed | tf_op | source)
XLA Modules:
  0.0 96.6 jit_solution(3527738131236864244)
XLA Ops:
  0.6 94.3 %policy_step.1 = (f32[64,256]{1,0:T(8,128)}, f32[64,512]{1,0:T(8,128)}, f32[8,128]{1,0:T(8,128)}, f32[24,128]{1,0:T(8,128)}) custom-call(bf16[1,256,3072]{2,1,0:T(8,128)(2,1)} %q_hbm.1, bf16[1,256,3072]{2,1,0:T(8,128)(2,1)} %k_hbm.1, bf16[1,256,3072]{2,1,0:T(8,128)(2,1)} %v_hbm.1, f32[64,256]{1,0:T(8,128)} %bitcast.17, f32[64,256]{1,0:T(8,128)} %bitcast.18, ...), custom_call_target="tpu_custom_call" | custom-call | flops 7000000000 | bytes 6000000 | tf_op jit(solution)/shard_map/policy_step/pallas_call | solution.py:514
  95.0 1.6 %hand_over.1 = (f32[64,256]{1,0:T(8,128)}, f32[64,512]{1,0:T(8,128)}, f32[16]{0:T(128)}, f32[24,128]{1,0:T(8,128)}) custom-call(f32[64,256]{1,0:T(8,128)} %get-tuple-element.12.next_in, f32[64,512]{1,0:T(8,128)} %get-tuple-element.13.learn_in, f32[8,128]{1,0:T(8,128)} %get-tuple-element.14.ratio_in, f32[24,128]{1,0:T(8,128)} %get-tuple-element.15.grad_in), custom_call_target="tpu_custom_call" | custom-call | tf_op jit(solution)/shard_map/hand_over/pallas_call | solution.py:580

commit v5 on v4

--- a/solution.py
+++ b/solution.py
@@ -51,8 +51,8 @@
     qland, kland, vland, att, prob, held, lat, noise, hw, up_ref, adv_ref, len_ref, time_ref, dest_ref,
     next_ref, learn_ref, ratio_ref, grad_ref,
     weight, early, early_square, piece, wg, cs_out, cs_in, csb, offs, placing,
-    r1s, r1r, r2, slots, learn_in, g_out, g_in,
-    loc_sem, s0, r0, sa, ra, sc, rc, s1, r1, s2, rr2, sl, rl, s3, r3,
+    r1s, r1r, vs, vr, r2, slots, learn_in, g_out, g_in,
+    loc_sem, s0, r0, sa, ra, sc, rc, s1, r1, s2, rr2, sv, rv, sl, rl, s3, r3,
 ):
     me = lax.axis_index("sp")
     vid = lax.axis_index("dp")
@@ -337,11 +337,13 @@
             square_high = square.astype(BF16).astype(F32)
             stats = jnp.where(row16 == 0, mean_high, jnp.where(row16 == 1, mean - mean_high, 0.0))
             stats = jnp.where(row16 == 2, square_high, jnp.where(row16 == 3, square - square_high, stats))
-            message = jnp.concatenate([whole[:CH], whole[CH : 2 * CH] - csb[NP] * mean, stats], axis=0).astype(BF16)
+            message = jnp.concatenate([whole[CH : 2 * CH] - csb[NP] * mean, stats], axis=0).astype(BF16)
             if n < NP:
+                vs[n, :, span] = whole[:CH].astype(BF16)
                 r1s[half, n] = message
                 part_copies[half][n].start()
             else:
+                vr[NP, :, span] = whole[:CH].astype(BF16)
                 r1r[half, NP] = message
 
     steps = [(half, pair) for half in range(2) for pair in range(NSP // 2)]
@@ -358,14 +360,13 @@
             c.wait_recv()
         span = slice(half * HALF, (half + 1) * HALF)
         parts = [r1r[half, i].astype(F32) for i in range(NP + 1)]
-        total = functools.reduce(jnp.add, [p[: 2 * CH] for p in parts])
-        means = [p[128:129] + p[129:130] for p in parts]
-        squares = [p[130:131] + p[131:132] for p in parts]
+        means = [p[CH : CH + 1] + p[CH + 1 : CH + 2] for p in parts]
+        squares = [p[CH + 2 : CH + 3] + p[CH + 3 : CH + 4] for p in parts]
         mean = functools.reduce(jnp.add, means) * (1.0 / NSP)
         gaps = [m - mean for m in means]
         variance = functools.reduce(jnp.add, squares) + FEAT * functools.reduce(jnp.add, [g * g for g in gaps])
         rstd = lax.rsqrt(variance * (1.0 / (FEAT * NSP)) + NORM_EPS)
-        inner = total[CH:]
+        inner = functools.reduce(jnp.add, [p[:CH] for p in parts])
         for i in range(NP + 1):
             inner = inner + csb[i] * gaps[i]
         delta = inner * rstd
@@ -394,7 +395,6 @@
         ]
         for c in copies:
             c.start()
-        next_ref[:, span] = (lat[:, span] - STEP * total[:CH]) + offset
         return delta.astype(BF16), copies
 
     delta_first, copies_first = own_tokens(0)
@@ -424,7 +424,19 @@
             ((next_ref, next_hbm), (learn_ref, learn_hbm), (ratio_ref, ratio_hbm), (grad_ref, grad_hbm))
         )
     ]
-    outward[0].start()
+    velocity_copies = [
+        pltpu.make_async_remote_copy(
+            src_ref=vs.at[i],
+            dst_ref=vr.at[i],
+            send_sem=sv.at[i],
+            recv_sem=rv.at[i],
+            device_id=(peer(i), vid),
+            device_id_type=MESH,
+        )
+        for i in range(NP)
+    ]
+    for c in velocity_copies:
+        c.start()
 
     def grad_part(half, s):
         u = r2[half, s, 0:CH]
@@ -477,6 +489,11 @@
     select = lax.broadcasted_iota(jnp.int32, (CH, HD), 0) == lax.broadcasted_iota(jnp.int32, (CH, HD), 1)
     learn_ref[...] = nt(select.astype(F32).astype(BF16), learn_in[...])
     outward[1].start()
+    for c in velocity_copies:
+        c.wait()
+    velocity = functools.reduce(jnp.add, [vr[i].astype(F32) for i in range(NP + 1)])
+    next_ref[...] = (lat[...] - STEP * velocity) + offs[...]
+    outward[0].start()
     for c in unit_copies[0] + unit_copies[1] + part_copies[0] + part_copies[1]:
         c.wait_send()
 
@@ -550,8 +567,10 @@
             pltpu.VMEM((NSP, CH, HD), F32),
             pltpu.VMEM((CH, ROWS), F32),
             pltpu.VMEM((512, ROWS), BF16),
-            pltpu.VMEM((2, NP, 144, HALF), BF16),
-            pltpu.VMEM((2, NSP, 144, HALF), BF16),
+            pltpu.VMEM((2, NP, CH + 16, HALF), BF16),
+            pltpu.VMEM((2, NSP, CH + 16, HALF), BF16),
+            pltpu.VMEM((NP, CH, ROWS), BF16),
+            pltpu.VMEM((NSP, CH, ROWS), BF16),
             pltpu.VMEM((2, NSP, CH + 16, HALF), BF16),
             pltpu.VMEM((512, HD), BF16),
             pltpu.VMEM((512, HD), BF16),
@@ -563,6 +582,7 @@
             dma((NP,)), dma((NP,)),
             dma((2, NP)), dma((2, NP)),
             dma((2, NP)), dma((2, NP)),
+            dma((NP,)), dma((NP,)),
             dma((NDP,)), dma((NDP,)),
             dma((NDP,)), dma((NDP,)),
         ],

time: 96.8 us -> 96.8 us (level)
  no operation moved by 1% of the time
where the time goes in v5:
time: 96.8 us; the launch traced here: 96.6 us
  Pallas kernels  95.9 us (99%)
    pallas_call x1, Pallas kernels, on_device(): pl.pallas_call(kernel, out_shape=(jax.ShapeDtypeStruct((CH, ROWS), F32),...  94.3 us

profile of v5, /device:TPU:1, one launch (start us, length us, event | category | flops | bytes accessed | tf_op | source)
XLA Modules:
  0.0 96.6 jit_solution(16861168579023568904)
XLA Ops:
  0.6 94.3 %policy_step.1 = (f32[64,256]{1,0:T(8,128)}, f32[64,512]{1,0:T(8,128)}, f32[8,128]{1,0:T(8,128)}, f32[24,128]{1,0:T(8,128)}) custom-call(bf16[1,256,3072]{2,1,0:T(8,128)(2,1)} %q_hbm.1, bf16[1,256,3072]{2,1,0:T(8,128)(2,1)} %k_hbm.1, bf16[1,256,3072]{2,1,0:T(8,128)(2,1)} %v_hbm.1, f32[64,256]{1,0:T(8,128)} %bitcast.17, f32[64,256]{1,0:T(8,128)} %bitcast.18, ...), custom_call_target="tpu_custom_call" | custom-call | flops 7000000000 | bytes 6000000 | tf_op jit(solution)/shard_map/policy_step/pallas_call | solution.py:531
  95.0 1.6 %hand_over.1 = (f32[64,256]{1,0:T(8,128)}, f32[64,512]{1,0:T(8,128)}, f32[16]{0:T(128)}, f32[24,128]{1,0:T(8,128)}) custom-call(f32[64,256]{1,0:T(8,128)} %get-tuple-element.12.next_in, f32[64,512]{1,0:T(8,128)} %get-tuple-element.13.learn_in, f32[8,128]{1,0:T(8,128)} %get-tuple-element.14.ratio_in, f32[24,128]{1,0:T(8,128)} %get-tuple-element.15.grad_in), custom_call_target="tpu_custom_call" | custom-call | tf_op jit(solution)/shard_map/hand_over/pallas_call | solution.py:600

commit v6 on v5

--- a/solution.py
+++ b/solution.py
@@ -149,7 +149,7 @@
         for c in groups[n]:
             c.wait_recv()
 
-    for n in range(3):
+    for n in range(2):
         issue(n)
     for c in local:
         c.start()
@@ -249,7 +249,7 @@
         c.wait()
     for n in range(3):
         sent(n)
-        issue(n + 3)
+        issue(n + 2)
     for n in range(3):
         arrived(n)
     attend_all(0)
@@ -276,7 +276,7 @@
     cs_in[NP] = cs_out[...]
     for n in range(3, 6):
         sent(n)
-        issue(n + 3)
+        issue(n + 2)
     for n in range(3, 6):
         arrived(n)
     attend_all(1)
@@ -287,6 +287,8 @@
         spread = jnp.transpose(jnp.broadcast_to(cs_in[i][0:1], (HD, HD)))
         csb[i] = spread[CH:]
 
+    sent(6)
+    issue(8)
     for n in (6, 7):
         arrived(n)
     attend_all(2)
@@ -352,7 +354,7 @@
         following = mix(*steps[n + 1]) if n + 1 < len(steps) else None
         partial_sums(*step, mixed)
         mixed = following
-    for n in (6, 7, 8):
+    for n in (7, 8):
         sent(n)
 
     def own_tokens(half):

time: 96.8 us -> 96.8 us (level)
  no operation moved by 1% of the time
where the time goes in v6:
time: 96.8 us; the launch traced here: 96.6 us
  Pallas kernels  96 us (99%)
    pallas_call x1, Pallas kernels, on_device(): pl.pallas_call(kernel, out_shape=(jax.ShapeDtypeStruct((CH, ROWS), F32),...  94.4 us

profile of v6, /device:TPU:1, one launch (start us, length us, event | category | flops | bytes accessed | tf_op | source)
XLA Modules:
  0.0 96.6 jit_solution(11278151375723501533)
XLA Ops:
  0.6 94.4 %policy_step.1 = (f32[64,256]{1,0:T(8,128)}, f32[64,512]{1,0:T(8,128)}, f32[8,128]{1,0:T(8,128)}, f32[24,128]{1,0:T(8,128)}) custom-call(bf16[1,256,3072]{2,1,0:T(8,128)(2,1)} %q_hbm.1, bf16[1,256,3072]{2,1,0:T(8,128)(2,1)} %k_hbm.1, bf16[1,256,3072]{2,1,0:T(8,128)(2,1)} %v_hbm.1, f32[64,256]{1,0:T(8,128)} %bitcast.17, f32[64,256]{1,0:T(8,128)} %bitcast.18, ...), custom_call_target="tpu_custom_call" | custom-call | flops 7000000000 | bytes 6000000 | tf_op jit(solution)/shard_map/policy_step/pallas_call | solution.py:533
  95.0 1.6 %hand_over.1 = (f32[64,256]{1,0:T(8,128)}, f32[64,512]{1,0:T(8,128)}, f32[16]{0:T(128)}, f32[24,128]{1,0:T(8,128)}) custom-call(f32[64,256]{1,0:T(8,128)} %get-tuple-element.12.next_in, f32[64,512]{1,0:T(8,128)} %get-tuple-element.13.learn_in, f32[8,128]{1,0:T(8,128)} %get-tuple-element.14.ratio_in, f32[24,128]{1,0:T(8,128)} %get-tuple-element.15.grad_in), custom_call_target="tpu_custom_call" | custom-call | tf_op jit(solution)/shard_map/hand_over/pallas_call | solution.py:602

commit v7 on v6

--- a/solution.py
+++ b/solution.py
@@ -119,7 +119,7 @@
 
     pl.semaphore_wait(barrier, NP + NDP - 1)
 
-    order = (0, 1, 2, 3, 4, 5, 7, 6, 8)
+    order = (0, 1, 2, 3, 4, 6, 7, 5, 8)
     groups = []
     for g in order:
         h, t = g // 3, g % 3
@@ -226,14 +226,17 @@
     def block(h, b, scores):
         rows = rows_of(b)
         chances = soften(scores)
-        if h == 2:
-            prob[rows, :] = chances
-            return
-        finish(h, rows, nn(chances, vland[h]))
-        if h == 1:
-            feature = att[rows, 0 : 2 * HD]
-            early[b] = nt(weight[:, 0 : 2 * HD], feature)
-            early_square[b] = squares_of(feature)[0:8]
+        if h > 0:
+            prob[h - 1, rows, :] = chances
+        else:
+            finish(0, rows, nn(chances, vland[0]))
+
+    def second_head(b):
+        rows = rows_of(b)
+        finish(1, rows, nn(prob[0, rows, :], vland[1]))
+        feature = att[rows, 0 : 2 * HD]
+        early[b] = nt(weight[:, 0 : 2 * HD], feature)
+        early_square[b] = squares_of(feature)[0:8]
 
     def attend_all(h):
         held[0] = score(h, rows_of(0))
@@ -274,10 +277,9 @@
     for c in cs_copies:
         c.start()
     cs_in[NP] = cs_out[...]
-    for n in range(3, 6):
+    for n in (3, 4):
         sent(n)
         issue(n + 2)
-    for n in range(3, 6):
         arrived(n)
     attend_all(1)
 
@@ -287,11 +289,18 @@
         spread = jnp.transpose(jnp.broadcast_to(cs_in[i][0:1], (HD, HD)))
         csb[i] = spread[CH:]
 
-    sent(6)
-    issue(8)
-    for n in (6, 7):
+    for n in (5, 6):
+        sent(n)
+        issue(n + 2)
         arrived(n)
     attend_all(2)
+    arrived(7)
+
+    @pl.loop(0, NSP // 2)
+    def _(pair):
+        second_head(2 * pair)
+        second_head(2 * pair + 1)
+
     arrived(8)
 
     owners = [peer(i) for i in range(NP)] + [me]
@@ -314,7 +323,7 @@
         return pl.ds(pl.multiple_of(s * ROWS + half * HALF, HALF), HALF)
 
     def mix(half, pair):
-        chances = [prob[tokens_of(owners[2 * pair + one], half), :] for one in range(2)]
+        chances = [prob[1, tokens_of(owners[2 * pair + one], half), :] for one in range(2)]
         return nn(jnp.concatenate(chances, axis=0), vland[2])
 
     row16 = lax.broadcasted_iota(jnp.int32, (16, HALF), 0)
@@ -545,7 +554,7 @@
             pltpu.VMEM((HEADS, SEQ, HD), BF16),
             pltpu.VMEM((HEADS, SEQ, 2 * HD), BF16),
             pltpu.VMEM((SEQ, FEAT), BF16),
-            pltpu.VMEM((SEQ, SEQ), BF16),
+            pltpu.VMEM((2, SEQ, SEQ), BF16),
             pltpu.VMEM((2, ROWS, SEQ), F32),
             pltpu.VMEM((CH, ROWS), F32),
             pltpu.VMEM((CH, ROWS), F32),

time: 96.8 us -> 96 us (level)
  no operation moved by 1% of the time
where the time goes in v7:
time: 96 us; the launch traced here: 95.8 us
  Pallas kernels  95.1 us (99%)
    pallas_call x1, Pallas kernels, on_device(): pl.pallas_call(kernel, out_shape=(jax.ShapeDtypeStruct((CH, ROWS), F32),...  93.5 us

profile of v7, /device:TPU:1, one launch (start us, length us, event | category | flops | bytes accessed | tf_op | source)
XLA Modules:
  0.0 95.8 jit_solution(9193222800485508041)
XLA Ops:
  0.6 93.5 %policy_step.1 = (f32[64,256]{1,0:T(8,128)}, f32[64,512]{1,0:T(8,128)}, f32[8,128]{1,0:T(8,128)}, f32[24,128]{1,0:T(8,128)}) custom-call(bf16[1,256,3072]{2,1,0:T(8,128)(2,1)} %q_hbm.1, bf16[1,256,3072]{2,1,0:T(8,128)(2,1)} %k_hbm.1, bf16[1,256,3072]{2,1,0:T(8,128)(2,1)} %v_hbm.1, f32[64,256]{1,0:T(8,128)} %bitcast.17, f32[64,256]{1,0:T(8,128)} %bitcast.18, ...), custom_call_target="tpu_custom_call" | custom-call | flops 7000000000 | bytes 6000000 | tf_op jit(solution)/shard_map/policy_step/pallas_call | solution.py:542
  94.2 1.6 %hand_over.1 = (f32[64,256]{1,0:T(8,128)}, f32[64,512]{1,0:T(8,128)}, f32[16]{0:T(128)}, f32[24,128]{1,0:T(8,128)}) custom-call(f32[64,256]{1,0:T(8,128)} %get-tuple-element.12.next_in, f32[64,512]{1,0:T(8,128)} %get-tuple-element.13.learn_in, f32[8,128]{1,0:T(8,128)} %get-tuple-element.14.ratio_in, f32[24,128]{1,0:T(8,128)} %get-tuple-element.15.grad_in), custom_call_target="tpu_custom_call" | custom-call | tf_op jit(solution)/shard_map/hand_over/pallas_call | solution.py:611

commit v8 on v7

--- a/solution.py
+++ b/solution.py
@@ -446,8 +446,6 @@
         )
         for i in range(NP)
     ]
-    for c in velocity_copies:
-        c.start()
 
     def grad_part(half, s):
         u = r2[half, s, 0:CH]
@@ -458,6 +456,9 @@
     for half in range(2):
         for i in range(NP):
             unit_copies[half][i].wait_recv()
+        if half == 1:
+            for c in velocity_copies:
+                c.start()
         for i in range(NP):
             grad = grad + grad_part(half, source(i))
     sides = r2[0, 0, CH : CH + 16].astype(F32) + r2[1, 0, CH : CH + 16].astype(F32)

time: 96 us -> 96.1 us (level)
  no operation moved by 1% of the time
where the time goes in v8:
time: 96.1 us; the launch traced here: 95.8 us
  Pallas kernels  95.2 us (99%)
    pallas_call x1, Pallas kernels, on_device(): pl.pallas_call(kernel, out_shape=(jax.ShapeDtypeStruct((CH, ROWS), F32),...  93.6 us

profile of v8, /device:TPU:1, one launch (start us, length us, event | category | flops | bytes accessed | tf_op | source)
XLA Modules:
  0.0 95.8 jit_solution(4881894992185180116)
XLA Ops:
  0.6 93.6 %policy_step.1 = (f32[64,256]{1,0:T(8,128)}, f32[64,512]{1,0:T(8,128)}, f32[8,128]{1,0:T(8,128)}, f32[24,128]{1,0:T(8,128)}) custom-call(bf16[1,256,3072]{2,1,0:T(8,128)(2,1)} %q_hbm.1, bf16[1,256,3072]{2,1,0:T(8,128)(2,1)} %k_hbm.1, bf16[1,256,3072]{2,1,0:T(8,128)(2,1)} %v_hbm.1, f32[64,256]{1,0:T(8,128)} %bitcast.17, f32[64,256]{1,0:T(8,128)} %bitcast.18, ...), custom_call_target="tpu_custom_call" | custom-call | flops 7000000000 | bytes 6000000 | tf_op jit(solution)/shard_map/policy_step/pallas_call | solution.py:543
  94.2 1.6 %hand_over.1 = (f32[64,256]{1,0:T(8,128)}, f32[64,512]{1,0:T(8,128)}, f32[16]{0:T(128)}, f32[24,128]{1,0:T(8,128)}) custom-call(f32[64,256]{1,0:T(8,128)} %get-tuple-element.12.next_in, f32[64,512]{1,0:T(8,128)} %get-tuple-element.13.learn_in, f32[8,128]{1,0:T(8,128)} %get-tuple-element.14.ratio_in, f32[24,128]{1,0:T(8,128)} %get-tuple-element.15.grad_in), custom_call_target="tpu_custom_call" | custom-call | tf_op jit(solution)/shard_map/hand_over/pallas_call | solution.py:612
